TPU v7x, 32 devices: a whole 2x2x4 slice. The times are simulated.
32 devices in a mesh: row: 4 (over y, x), col: 4 (over z), layer: 2 (over core).
Axes of the slice: x: 2, y: 2, z: 4, core: 2. Of those that a mesh axis runs over, the one named last changes fastest.
Arguments:
- density: bfloat16 [4096, 4096], P('row', ('col', 'layer')), as said below
- cotangent: bfloat16 [4096, 4096], P('row', ('col', 'layer')), may hold values from -6 to 6
- block_pattern: int32 [2, 362], replicated, may hold values from 0 to 31, as said below
Outputs:
- gradient: float32 [4096, 4096], P('row', ('col', 'layer'))
Inputs may be any that keep to these rules, and one draw needn't show every extreme that they name: `block_pattern`: each column names one nonzero block; no block is named twice; every block (c, r) is listed with (r, c); all 32 diagonal blocks are listed, and 165 blocks above the diagonal. density is symmetric.
All inputs are finite; a program needn't handle non-finite values.
Results may differ from a plain program's by a relative error of at most 0.0025.
Values may be sent and summed in bfloat16 or wider, within the bound.
A program may use at most 128 MiB of HBM per device.

v0:
```python
import jax
import jax.numpy as jnp
from jax import lax
from jax.sharding import PartitionSpec as P

BS = 128


def rows_of(matrix):
    return lax.all_gather(matrix, ("col", "layer"), axis=1, tiled=True)


def times_right(left_rows, right_tile):
    return jnp.dot(
        left_rows,
        lax.all_gather(right_tile, "row", axis=0, tiled=True),
        preferred_element_type=jnp.float32,
    )


def per_device(density, cotangent, block_pattern):
    tile_rows, tile_cols = density.shape
    row_start = lax.axis_index("row") * tile_rows
    col_start = lax.axis_index(("col", "layer")) * tile_cols
    row_block = (row_start + jnp.arange(tile_rows, dtype=jnp.int32)) // BS
    col_block = (col_start + jnp.arange(tile_cols, dtype=jnp.int32)) // BS
    row_hits = (block_pattern[0][:, None] == row_block[None, :]).astype(jnp.bfloat16)
    col_hits = (block_pattern[1][:, None] == col_block[None, :]).astype(jnp.bfloat16)
    counted = jnp.einsum("nr,nc->rc", row_hits, col_hits, preferred_element_type=jnp.float32)
    mask = counted > 0.5
    xm = jnp.where(mask, density, jnp.zeros_like(density))
    masked_grad = jnp.where(mask, cotangent, jnp.zeros_like(cotangent))
    square = jnp.where(mask, times_right(rows_of(xm), xm), 0.0).astype(jnp.bfloat16)
    grad_times = times_right(rows_of(masked_grad), xm)
    pulled = jnp.where(mask, 3.0 * masked_grad.astype(jnp.float32) - 2.0 * grad_times, 0.0).astype(
        jnp.bfloat16
    )
    first_term = times_right(rows_of(square), masked_grad)
    second_term = times_right(rows_of(pulled), xm)
    third_term = times_right(rows_of(xm), pulled)
    return jnp.where(mask, -2.0 * first_term + second_term + third_term, 0.0)


def solution(mesh):
    in_specs = (P("row", ("col", "layer")), P("row", ("col", "layer")), P())
    out_specs = P("row", ("col", "layer"))
    return jax.shard_map(
        per_device, mesh=mesh, in_specs=in_specs, out_specs=out_specs, check_vma=False
    )
```

profile of v0, /device:TPU:0, one launch (start us, length us, event | category | flops | bytes accessed | tf_op | source)
XLA Modules:
  0.0 524.9 jit_solution(15661243915619731962)
XLA Ops:
  6.5 0.0 all-gather.10.cloned.1.call-start
  6.6 0.8 slice_reduce_fusion
  7.3 0.0 copy-start
  7.4 4.2 broadcast_select_fusion
  11.6 0.0 all-gather.10.cloned.1.call-update
  11.6 0.0 all-gather.16.cloned.1.call-start
  11.6 0.7 all-gather.16.cloned.1.call-update
  12.3 0.0 all-gather.8.cloned.1.call-start
  12.4 0.7 all-gather.8.cloned.1.call-update
  13.1 0.0 all-gather.20.cloned.1.call-start
  13.1 54.0 %all-gather.10.cloned.1.call-done = bf16[4096,512]{1,0:T(8,128)(2,1)} async-done(((bf16[1024,512]{1,0:T(8,128)(2,1)}), bf16[4096,512]{1,0:T(8,128)(2,1)}) %all-gather.10.cloned.1.call-update) | async-done | bytes 4194320 | tf_op jit(solution)/shard_map/all_gather | solution.py:16
  67.1 83.7 %all-gather.16.cloned.1.call-done = bf16[1024,4096]{1,0:T(8,128)(2,1)} async-done(((bf16[1024,512]{1,0:T(8,128)(2,1)}), bf16[1024,4096]{1,0:T(8,128)(2,1)}) %all-gather.16.cloned.1.call-update) | async-done | bytes 8388624 | tf_op jit(solution)/shard_map/all_gather | solution.py:10
  150.8 0.0 copy-done
  150.8 10.3 %select_convert_fusion = bf16[1024,512]{1,0:T(8,128)(2,1)} fusion(pred[1024,512]{1,0:T(32,128)(4,1)S(1)} %get-tuple-element.9, bf16[1024,4096]{1,0:T(8,128)(2,1)} %all-gather.16.cloned.1.call-done, bf16[4096,512]{1,0:T(8,128)(2,1)} %all-gather.10.cloned.1.call-done, bf16[1024,512]{1,0:T(8,128)(2,1)S(1)} %copy-done), kind=kOutput, calls=%fused_computation.1 | convolution fusion | flops 4298637312 | bytes 15204352 | tf_op jit(solution)/shard_map/dot_general | solution.py:14
  161.1 0.0 all-gather.20.cloned.1.call-update
  161.2 0.0 all-gather.18.cloned.1.call-start
  161.2 0.5 all-gather.18.cloned.1.call-update
  161.7 0.0 all-gather.14.cloned.1.call-start
  161.8 0.5 all-gather.14.cloned.1.call-update
  162.3 0.2 all-gather.12.cloned.1.call-start
  162.6 70.5 %all-gather.8.cloned.1.call-done = bf16[1024,4096]{1,0:T(8,128)(2,1)} async-done(((bf16[1024,512]{1,0:T(8,128)(2,1)}), bf16[1024,4096]{1,0:T(8,128)(2,1)}) %all-gather.8.cloned.1.call-update) | async-done | bytes 8388624 | tf_op jit(solution)/shard_map/all_gather | solution.py:10
  233.1 10.0 %select_convert_fusion.1 = bf16[1024,512]{1,0:T(8,128)(2,1)} fusion(pred[1024,512]{1,0:T(32,128)(4,1)S(1)} %get-tuple-element.9, bf16[1024,4096]{1,0:T(8,128)(2,1)} %all-gather.8.cloned.1.call-done, bf16[4096,512]{1,0:T(8,128)(2,1)} %all-gather.10.cloned.1.call-done), kind=kOutput, calls=%fused_computation.2 | convolution fusion | flops 4296015872 | bytes 14155776 | tf_op jit(solution)/shard_map/dot_general | solution.py:14
  243.1 0.0 all-gather.12.cloned.1.call-update
  243.1 42.9 %all-gather.20.cloned.1.call-done = bf16[4096,512]{1,0:T(8,128)(2,1)} async-done(((bf16[1024,512]{1,0:T(8,128)(2,1)}), bf16[4096,512]{1,0:T(8,128)(2,1)}) %all-gather.20.cloned.1.call-update) | async-done | bytes 4194320 | tf_op jit(solution)/shard_map/all_gather | solution.py:16
  286.0 10.4 %fusion.17 = f32[1024,512]{1,0:T(8,128)} fusion(bf16[1024,4096]{1,0:T(8,128)(2,1)} %all-gather.8.cloned.1.call-done, bf16[4096,512]{1,0:T(8,128)(2,1)} %all-gather.20.cloned.1.call-done), kind=kOutput, calls=%fused_computation.34 | convolution fusion | flops 4294967296 | bytes 14680064 | tf_op jit(solution)/shard_map/dot_general | solution.py:14
  296.4 73.2 %all-gather.18.cloned.1.call-done = bf16[1024,4096]{1,0:T(8,128)(2,1)} async-done(((bf16[1024,512]{1,0:T(8,128)(2,1)}), bf16[1024,4096]{1,0:T(8,128)(2,1)}) %all-gather.18.cloned.1.call-update) | async-done | bytes 8388624 | tf_op jit(solution)/shard_map/all_gather | solution.py:10
  369.6 10.4 %fusion.16 = f32[1024,512]{1,0:T(8,128)} fusion(bf16[1024,4096]{1,0:T(8,128)(2,1)} %all-gather.18.cloned.1.call-done, bf16[4096,512]{1,0:T(8,128)(2,1)} %all-gather.10.cloned.1.call-done), kind=kOutput, calls=%fused_computation.33 | convolution fusion | flops 4294967296 | bytes 14680064 | tf_op jit(solution)/shard_map/dot_general | solution.py:14
  380.0 42.6 %all-gather.14.cloned.1.call-done = bf16[4096,512]{1,0:T(8,128)(2,1)} async-done(((bf16[1024,512]{1,0:T(8,128)(2,1)}), bf16[4096,512]{1,0:T(8,128)(2,1)}) %all-gather.14.cloned.1.call-update) | async-done | bytes 4194320 | tf_op jit(solution)/shard_map/all_gather | solution.py:16
  422.6 83.7 %all-gather.12.cloned.1.call-done = bf16[1024,4096]{1,0:T(8,128)(2,1)} async-done(((bf16[1024,512]{1,0:T(8,128)(2,1)}), bf16[1024,4096]{1,0:T(8,128)(2,1)}) %all-gather.12.cloned.1.call-update) | async-done | bytes 8388624 | tf_op jit(solution)/shard_map/all_gather | solution.py:10
  506.2 11.8 %add_select_fusion = f32[1024,512]{1,0:T(8,128)} fusion(pred[1024,512]{1,0:T(32,128)(4,1)S(1)} %get-tuple-element.9, f32[1024,512]{1,0:T(8,128)} %fusion.17, f32[1024,512]{1,0:T(8,128)} %fusion.16, bf16[1024,4096]{1,0:T(8,128)(2,1)} %all-gather.12.cloned.1.call-done, bf16[4096,512]{1,0:T(8,128)(2,1)} %all-gather.14.cloned.1.call-done), kind=kOutput, calls=%fused_computation | convolution fusion | flops 4297064448 | bytes 19398656 | tf_op jit(solution)/shard_map/dot_general | solution.py:14
  (2 shorter events, 0.0 us)
Async XLA Ops:
  6.5 60.6 %all-gather.10.cloned.1.call-start = ((), (), s32[]{:S(2)}) async-start(), calls=%async_computation.1 | async-start | bytes 5242880 | tf_op jit(solution)/shard_map/all_gather | solution.py:16
  7.3 143.5 %copy-start = (bf16[1024,512]{1,0:T(8,128)(2,1)S(1)}, bf16[1024,512]{1,0:T(8,128)(2,1)}, u32[]{:S(2)}) copy-start(bf16[1024,512]{1,0:T(8,128)(2,1)} %param.4) | copy-start | bytes 3145732
  11.6 139.3 %all-gather.16.cloned.1.call-start = ((), (), s32[]{:S(2)}) async-start(), calls=%async_computation.4 | async-start | bytes 9437184 | tf_op jit(solution)/shard_map/all_gather | solution.py:10
  12.3 220.7 %all-gather.8.cloned.1.call-start = ((), (), s32[]{:S(2)}) async-start(), calls=%async_computation | async-start | bytes 9437184 | tf_op jit(solution)/shard_map/all_gather | solution.py:10
  13.1 273.0 %all-gather.20.cloned.1.call-start = ((), (), s32[]{:S(2)}) async-start(), calls=%async_computation.6 | async-start | bytes 5242880 | tf_op jit(solution)/shard_map/all_gather | solution.py:16
  161.2 208.4 %all-gather.18.cloned.1.call-start = ((), (), s32[]{:S(2)}) async-start(), calls=%async_computation.5 | async-start | bytes 9437184 | tf_op jit(solution)/shard_map/all_gather | solution.py:10
  161.7 260.8 %all-gather.14.cloned.1.call-start = ((), (), s32[]{:S(2)}) async-start(), calls=%async_computation.3 | async-start | bytes 5242880 | tf_op jit(solution)/shard_map/all_gather | solution.py:16
  162.3 343.9 %all-gather.12.cloned.1.call-start = ((), (), s32[]{:S(2)}) async-start(), calls=%async_computation.2 | async-start | bytes 9437184 | tf_op jit(solution)/shard_map/all_gather | solution.py:10
Sparse Core Ops, SparseCore 0:
  11.7 55.3 all-gather.9
  68.7 82.0 all-gather.15
  152.4 80.5 all-gather.7
  234.8 51.2 all-gather.19
  287.5 82.0 all-gather.17
  371.3 51.2 all-gather.13
  424.2 82.0 all-gather.11
where the time goes:
time: 525 us
  waiting for transfers between devices  453 us (86%)
  matrix products  57.1 us (11%)
  between operations  13.5 us (3%)
    all_gather x4, waiting for transfers between devices, rows_of(): return lax.all_gather(matrix, ('col', 'layer'), axis=1, tiled=True)  311 us
    all_gather x3, waiting for transfers between devices, times_right(): lax.all_gather(right_tile, 'row', axis=0, tiled=True)  140 us
    dot_general x5, matrix products, times_right(): jnp.dot(left_rows, lax.all_gather(right_tile, 'row', axis=0, tiled=True),...  52.9 us
  transfers between devices with their start and end apart: 7, of which 7 were waited for; matrix products, arithmetic and copies ran while one was open for 8% of the time, Pallas kernels for 0%

commit v1 on v0

v1 whole, which is shorter than its diff:
```python
import jax
import jax.numpy as jnp
from jax import lax
from jax.experimental import pallas as pl
from jax.experimental.pallas import tpu as pltpu
from jax.sharding import PartitionSpec as P

BS = 128
MESH = pl.DeviceIdType.MESH
ANY = pl.BlockSpec(memory_space=pl.ANY)


def ring_place(index, size):
    upper = index // (size // 2)
    return index + upper * (size + size // 2 - 1 - 2 * index)


class Spot:
    def __init__(self, rows, cols):
        self.rows, self.cols = rows, cols
        self.r = lax.axis_index("row")
        self.c = lax.axis_index("col")
        self.l = lax.axis_index("layer")
        self.p = ring_place(self.r, rows)
        self.right = (self.at(1), self.c, self.l)
        self.left = (self.at(-1), self.c, self.l)
        self.sibling = (self.r, self.c, 1 - self.l)
        self.up = (self.r, lax.rem(self.c + 1, cols), self.l)
        self.down = (self.r, lax.rem(self.c + cols - 1, cols), self.l)

    def at(self, step):
        return ring_place(lax.rem(self.p + step + self.rows, self.rows), self.rows)

    def greet(self, others):
        barrier = pltpu.get_barrier_semaphore()
        for other in others:
            pl.semaphore_signal(barrier, inc=1, device_id=other, device_id_type=MESH)
        pl.semaphore_wait(barrier, len(others))


def remote(src, dst, send, recv, device):
    return pltpu.make_async_remote_copy(
        src_ref=src, dst_ref=dst, send_sem=send, recv_sem=recv, device_id=device, device_id_type=MESH
    )


def ring_copies(spot, view, own, sends, recvs, item):
    half_way = spot.rows // 2
    tile = own.shape[0]
    steps = []
    for step in range(1, half_way + 1):
        pair = []
        for way, (target, sign) in enumerate(((spot.right, 1), (spot.left, -1))):
            origin = spot.at(-sign * (step - 1))
            if step < half_way:
                first, count = 0, tile
            else:
                first, count = way * (tile // 2), tile // 2
            src = own.at[pl.ds(first, count), :] if step == 1 else view(origin, first, count)
            pair.append(
                remote(
                    src,
                    view(origin, first, count),
                    sends.at[item, step - 1, way],
                    recvs.at[item, step - 1, way],
                    target,
                )
            )
        steps.append(pair)
    return steps


def gather_kernel(rows, cols, x_ref, g_ref, xr, xh, gr, gc, zs, zr, rs, rr, ss, sr, ls):
    spot = Spot(rows, cols)
    height, width = x_ref.shape
    c, l = spot.c, spot.l

    def wide(ref, col):
        return ref.at[:, pl.ds(pl.multiple_of((col * 2 + l) * width, width), width)]

    def x_view(col):
        def view(row, first, count):
            return xh.at[
                pl.ds(pl.multiple_of(row * height + first, 16), count),
                pl.ds(pl.multiple_of(col * width, width), width),
            ]

        return view

    def g_view(row, first, count):
        return gc.at[pl.ds(pl.multiple_of(row * height + first, 16), count), :]

    def x_mine(col):
        return x_view(col)(spot.r, 0, height)

    spot.greet((spot.right, spot.left, spot.sibling, spot.up, spot.down))

    items = [(0, 0)] + [(way, d) for d in range(1, cols) for way in (0, 1)]
    index_of = {item: i for i, item in enumerate(items)}

    def col_of(item):
        way, d = item
        return c - d if way == 0 else c + d

    def there(item):
        way, d = item
        if d == 0:
            return None
        return c >= d if way == 0 else c < cols - d

    def when(cond, body):
        if cond is None:
            body()
        else:
            pl.when(cond)(body)

    def both(a, b):
        return b if a is None else jnp.logical_and(a, b)

    def line_copy(kind, way, d):
        col = c - d if way == 0 else c + d
        own, view = (x_ref, x_mine) if kind == 0 else (g_ref, lambda k: wide(gr, k))
        src = own if d == 0 else view(col)
        target = spot.up if way == 0 else spot.down
        return remote(src, view(col), zs.at[kind, way, d], zr.at[kind, way, d], target)

    def line_sends(way, d):
        further = c < cols - 1 if way == 0 else c > 0
        return both(there((way, d)), further)

    def sibling_copy(kind, item):
        i = index_of[item]
        col = col_of(item)
        if kind == 0:
            src = x_ref if i == 0 else x_mine(col)
            dst = wide(xr, col)
        else:
            src = g_ref if i == 0 else wide(gr, col)
            dst = wide(gr, col)
        return remote(src, dst, ss.at[kind, i], sr.at[kind, i], spot.sibling)

    def sibling_arrival(kind, item):
        return sibling_copy(kind, item)

    def local_copy(item):
        i = index_of[item]
        col = col_of(item)
        src = x_ref if i == 0 else x_mine(col)
        return pltpu.make_async_copy(src, wide(xr, col), ls.at[i])

    def x_ring(item):
        return ring_copies(
            spot, x_view(col_of(item)), x_ref if item[1] == 0 else x_mine_ref(item), rs, rr, index_of[item]
        )

    def x_mine_ref(item):
        return x_mine(col_of(item))

    g_item = len(items)

    def g_ring():
        return ring_copies(spot, g_view, g_ref, rs, rr, g_item)

    def own_copies():
        return [
            pltpu.make_async_copy(x_ref, x_mine(c), ls.at[len(items)]),
            pltpu.make_async_copy(g_ref, wide(gr, c), ls.at[len(items) + 1]),
            pltpu.make_async_copy(g_ref, g_view(spot.r, 0, height), ls.at[len(items) + 2]),
        ]

    def start_pair(pair):
        for copy in pair:
            copy.start()

    def forward(steps, step):
        for way in (0, 1):
            steps[step - 1][way].wait_recv()
        start_pair(steps[step])

    ring_steps = rows // 2

    for way in (0, 1):
        when(line_sends(way, 0), lambda way=way: line_copy(0, way, 0).start())
    start_pair(x_ring((0, 0))[0])
    start_pair(g_ring()[0])
    for copy in own_copies():
        copy.start()
    for kind in (0, 1):
        sibling_copy(kind, (0, 0)).start()
    local_copy((0, 0)).start()
    for way in (0, 1):
        when(line_sends(way, 0), lambda way=way: line_copy(1, way, 0).start())

    def arrive_x(item):
        way, d = item
        line_copy(0, way, d - 1).wait_recv()
        when(line_sends(way, d) if d < cols - 1 else jnp.bool_(False), lambda: line_copy(0, way, d).start())
        start_pair(x_ring(item)[0])
        sibling_copy(0, item).start()
        local_copy(item).start()

    def arrive_g(item):
        way, d = item
        line_copy(1, way, d - 1).wait_recv()
        when(line_sends(way, d) if d < cols - 1 else jnp.bool_(False), lambda: line_copy(1, way, d).start())
        sibling_copy(1, item).start()

    def ring_on(item):
        steps = x_ring(item)
        for step in range(1, ring_steps):
            forward(steps, step)

    def g_ring_on():
        steps = g_ring()
        for step in range(1, ring_steps):
            forward(steps, step)

    for d in range(1, cols):
        for way in (0, 1):
            when(there((way, d)), lambda way=way, d=d: arrive_x((way, d)))
        if d == 1:
            ring_on((0, 0))
            g_ring_on()
        else:
            for way in (0, 1):
                when(there((way, d - 1)), lambda way=way, d=d: ring_on((way, d - 1)))
        for way in (0, 1):
            when(there((way, d)), lambda way=way, d=d: arrive_g((way, d)))
    for way in (0, 1):
        when(there((way, cols - 1)), lambda way=way: ring_on((way, cols - 1)))

    def finish(item):
        way, d = item
        steps = x_ring(item)
        for step in range(ring_steps):
            for copy in steps[step]:
                copy.wait_send()
        for copy in steps[-1]:
            copy.wait_recv()
        for kind in (0, 1):
            sibling_copy(kind, item).wait_send()
            sibling_copy(kind, item).wait_recv()
        local_copy(item).wait()

    for item in items:
        when(there(item), lambda item=item: finish(item))
    steps = g_ring()
    for step in range(ring_steps):
        for copy in steps[step]:
            copy.wait_send()
    for copy in steps[-1]:
        copy.wait_recv()
    for copy in own_copies():
        copy.wait()
    for kind in (0, 1):
        for way in (0, 1):
            for d in range(cols - 1):
                when(line_sends(way, d), lambda kind=kind, way=way, d=d: line_copy(kind, way, d).wait_send())


def share_kernel(rows, cols, width, s_ref, p_ref, sf, pf, pc, rs, rr, ss, sr, ls):
    spot = Spot(rows, cols)
    height = s_ref.shape[0]
    spot.greet((spot.right, spot.left, spot.sibling))
    mine = p_ref.at[:, pl.ds(pl.multiple_of(spot.c * width, width), width)]

    def view(row, first, count):
        return pc.at[pl.ds(pl.multiple_of(row * height + first, 16), count), :]

    steps = ring_copies(spot, view, mine, rs, rr, 0)
    for copy in steps[0]:
        copy.start()
    others = [pltpu.make_async_copy(mine, view(spot.r, 0, height), ls.at[2 * cols])]
    for kind, (half, full) in enumerate(((p_ref, pf), (s_ref, sf))):
        for col in range(cols):
            src = half.at[:, pl.ds(col * width, width)]
            dst = full.at[:, pl.ds(pl.multiple_of((col * 2 + spot.l) * width, width), width)]
            others.append(remote(src, dst, ss.at[kind, col], sr.at[kind, col], spot.sibling))
            others.append(pltpu.make_async_copy(src, dst, ls.at[kind * cols + col]))
    for copy in others:
        copy.start()
    for step in range(1, len(steps)):
        for copy in steps[step - 1]:
            copy.wait_recv()
        for copy in steps[step]:
            copy.start()
    for copy in steps[-1]:
        copy.wait_recv()
    for pair in steps:
        for copy in pair:
            copy.wait_send()
    for copy in others:
        copy.wait()


def gather_all(rows, cols, x, g):
    height, width = x.shape
    shape = lambda a, b: jax.ShapeDtypeStruct((a, b), x.dtype)
    items = 2 * cols - 1
    dma = pltpu.SemaphoreType.DMA
    return pl.pallas_call(
        lambda *refs: gather_kernel(rows, cols, *refs),
        out_shape=(
            shape(height, 2 * cols * width),
            shape(rows * height, cols * width),
            shape(height, 2 * cols * width),
            shape(rows * height, width),
        ),
        in_specs=[ANY] * 2,
        out_specs=(ANY,) * 4,
        scratch_shapes=[
            dma((2, 2, cols)),
            dma((2, 2, cols)),
            dma((items + 1, rows // 2, 2)),
            dma((items + 1, rows // 2, 2)),
            dma((2, items)),
            dma((2, items)),
            dma((items + 3,)),
        ],
        compiler_params=pltpu.CompilerParams(collective_id=0, has_side_effects=True),
        name="gather_all",
    )(x, g)


def share(rows, cols, width, s, p):
    height = s.shape[0]
    shape = lambda a, b: jax.ShapeDtypeStruct((a, b), s.dtype)
    dma = pltpu.SemaphoreType.DMA
    return pl.pallas_call(
        lambda *refs: share_kernel(rows, cols, width, *refs),
        out_shape=(
            shape(height, 2 * cols * width),
            shape(height, 2 * cols * width),
            shape(rows * height, width),
        ),
        in_specs=[ANY] * 2,
        out_specs=(ANY,) * 3,
        scratch_shapes=[
            dma((1, rows // 2, 2)),
            dma((1, rows // 2, 2)),
            dma((2, cols)),
            dma((2, cols)),
            dma((2 * cols + 1,)),
        ],
        compiler_params=pltpu.CompilerParams(collective_id=1, has_side_effects=True),
        name="share",
    )(s, p)


def dot(a, b):
    return jnp.dot(a, b, preferred_element_type=jnp.float32)


def hits(blocks, positions):
    return (blocks[:, None] == positions[None, :] // BS).astype(jnp.bfloat16)


def mask_of(block_pattern, row_positions, col_positions):
    counted = jnp.einsum(
        "nr,nc->rc",
        hits(block_pattern[0], row_positions),
        hits(block_pattern[1], col_positions),
        preferred_element_type=jnp.float32,
    )
    return counted > 0.5


def solution(mesh):
    rows, cols, layers = mesh.shape["row"], mesh.shape["col"], mesh.shape["layer"]

    def per_device(density, cotangent, block_pattern):
        height, width = density.shape
        r, c, l = (lax.axis_index(name) for name in ("row", "col", "layer"))
        row_at = r * height + jnp.arange(height, dtype=jnp.int32)
        col_at = (c * layers + l) * width + jnp.arange(width, dtype=jnp.int32)
        along = jnp.arange(cols * width, dtype=jnp.int32)
        half_at = ((along // width) * layers + l) * width + along % width
        mask = mask_of(block_pattern, row_at, col_at)
        half_mask = mask_of(block_pattern, row_at, half_at)
        xm = jnp.where(mask, density, jnp.zeros_like(density))
        masked_grad = jnp.where(mask, cotangent, jnp.zeros_like(cotangent))
        x_rows, x_half, g_rows, g_cols = gather_all(rows, cols, xm, masked_grad)
        g_half = lax.dynamic_index_in_dim(
            g_rows.reshape(height, cols, layers, width), l, axis=2, keepdims=False
        ).reshape(height, cols * width)
        square = jnp.where(half_mask, dot(x_rows, x_half), 0.0).astype(jnp.bfloat16)
        pulled = jnp.where(
            half_mask, 3.0 * g_half.astype(jnp.float32) - 2.0 * dot(g_rows, x_half), 0.0
        ).astype(jnp.bfloat16)
        s_rows, p_rows, p_cols = share(rows, cols, width, square, pulled)
        x_cols = lax.dynamic_slice_in_dim(x_half, c * width, width, axis=1)
        total = -2.0 * dot(s_rows, g_cols) + dot(p_rows, x_cols) + dot(x_rows, p_cols)
        return jnp.where(mask, total, 0.0)

    return jax.shard_map(
        per_device,
        mesh=mesh,
        in_specs=(P("row", ("col", "layer")), P("row", ("col", "layer")), P()),
        out_specs=P("row", ("col", "layer")),
        check_vma=False,
    )
```

time: 525 us -> 635 us (1.21)
  Pallas kernels: 0 us -> 519 us
  waiting for transfers between devices: 453 us -> 0 us
  local copies, waits for them, and re-layouts: 0.79 us -> 33.8 us
  matrix products: 57.1 us -> 73.7 us
  between operations: 13.5 us -> 0.13 us
  other arithmetic: 0.02 us -> 8.79 us
    pallas_call x0 -> x2, Pallas kernels: none -> 519 us  [the longest x1 289 us: share(): pl.pallas_call(lambda *refs: share_kernel(rows, cols, width, *refs), out_...]
    all_gather x7 -> x0, waiting for transfers between devices: 451 us -> none  [the longest x4 311 us: rows_of(): return lax.all_gather(matrix, ('col', 'layer'), axis=1, tiled=True)]
    dot_general x6 -> x7, matrix products: 57.1 us -> 73.7 us  [the longest x5 65.3 us: dot(): return jnp.dot(a, b, preferred_element_type=jnp.float32)]
    reshape x0 -> x1, local copies, waits for them, and re-layouts: none -> 14.5 us  [per_device(): g_rows.reshape(height, cols, layers, width)]
    dynamic_slice x0 -> x1, local copies, waits for them, and re-layouts: none -> 10.9 us  [per_device(): lax.dynamic_index_in_dim(g_rows.reshape(height, cols, layers, width), l,...]
    mul x0 -> x1, other arithmetic: none -> 8.75 us  [per_device(): 3.0 * g_half.astype(jnp.float32) - 2.0 * dot(g_rows, x_half)]
    unnamed x2 -> x15, local copies, waits for them, and re-layouts: 0.01 us -> 7.69 us
  transfers between devices with their start and end apart: 7 -> 0, of which waited for: 7 -> 0; matrix products, arithmetic and copies ran while one was open for 8% -> 0% of each run, Pallas kernels for 0% -> 0%
where the time goes in v1:
time: 635 us
  Pallas kernels  519 us (82%)
  matrix products  73.7 us (12%)
  local copies, waits for them, and re-layouts  33.8 us (5%)
  other arithmetic  8.79 us (1%)
    pallas_call x1, Pallas kernels, share(): pl.pallas_call(lambda *refs: share_kernel(rows, cols, width, *refs), out_...  289 us
    pallas_call x1, Pallas kernels, gather_all(): pl.pallas_call(lambda *refs: gather_kernel(rows, cols, *refs), out_shape=...  230 us
    dot_general x5, matrix products, dot(): return jnp.dot(a, b, preferred_element_type=jnp.float32)  65.3 us
    reshape x1, local copies, waits for them, and re-layouts, per_device(): g_rows.reshape(height, cols, layers, width)  14.5 us

profile of v1, /device:TPU:0, one launch (start us, length us, event | category | flops | bytes accessed | tf_op | source)
XLA Modules:
  0.0 634.9 jit_solution(14436382980158268528)
XLA Ops:
  0.0 0.8 slice_reduce_fusion
  0.8 4.1 broadcast_select_fusion
  4.9 229.7 %gather_all.1 = (bf16[1024,4096]{1,0:T(8,128)(2,1)}, bf16[4096,2048]{1,0:T(8,128)(2,1)}, bf16[1024,4096]{1,0:T(8,128)(2,1)}, bf16[4096,512]{1,0:T(8,128)(2,1)}) custom-call(bf16[1024,512]{1,0:T(8,128)(2,1)} %get-tuple-element.22.refs_0_, bf16[1024,512]{1,0:T(8,128)(2,1)} %get-tuple-element.21.refs_1_), custom_call_target="tpu_custom_call" | custom-call | tf_op jit(solution)/shard_map/gather_all/pallas_call | solution.py:301
  234.7 14.5 %reshape.141 = bf16[1024,4,2,512]{3,2,1,0:T(2,128)(2,1)} reshape(bf16[1024,4096]{1,0:T(8,128)(2,1)} %get-tuple-element.14) | data formatting | bytes 16777216 | tf_op jit(solution)/shard_map/reshape | solution.py:384
  249.1 10.9 %constant_dynamic-slice_fusion = bf16[1024,4,1,512]{3,2,1,0:T(2,128)(2,1)} fusion(bf16[1024,4,2,512]{3,2,1,0:T(2,128)(2,1)} %reshape.141, s32[]{:T(128)S(6)} %select_n.84), kind=kLoop, calls=%fused_computation.66 | loop fusion | bytes 8388612 | tf_op jit(solution)/shard_map/jit(dynamic_index_in_dim)/dynamic_slice | solution.py:383
  260.0 8.8 %convert_multiply_fusion = f32[1024,4,1,512]{3,1,0,2:T(4,128)} fusion(bf16[1024,4,1,512]{3,2,1,0:T(2,128)(2,1)} %constant_dynamic-slice_fusion), kind=kLoop, calls=%fused_computation.1 | loop fusion | flops 4194304 | bytes 12582912 | tf_op jit(solution)/shard_map/mul | solution.py:388
  268.8 0.0 slice-start
  268.8 7.7 %copy.6 = f32[128,8,4,512]{3,1,2,0:T(8,128)S(1)} copy(f32[128,8,4,512]{3,2,1,0:T(4,128)} %bitcast.13) | data formatting | bytes 16777216
  276.5 0.0 slice-start.1
  276.5 0.0 slice-start.2
  276.5 4.3 broadcast_compare_fusion
  280.7 0.0 slice-done
  280.8 0.0 slice-done.1
  280.8 0.0 slice-start.3
  280.8 22.3 %select_convert_fusion.refs_1_ = bf16[1024,2048]{1,0:T(8,128)(2,1)} fusion(pred[1024,2048]{1,0:T(32,128)(4,1)} %broadcast_compare_fusion, f32[1024,2048]{1,0:T(8,128)S(1)} %bitcast.16, bf16[1024,4096]{1,0:T(8,128)(2,1)S(1)} %bitcast.15, bf16[4096,2048]{1,0:T(8,128)(2,1)} %get-tuple-element.13), kind=kOutput, calls=%fused_computation | convolution fusion | flops 17188257792 | bytes 39845888 | tf_op jit(solution)/shard_map/dot_general | solution.py:351
  303.1 0.0 slice-done.2
  303.1 0.0 slice-done.3
  303.1 21.4 %select_convert_fusion.1.refs_0_ = bf16[1024,2048]{1,0:T(8,128)(2,1)} fusion(pred[1024,2048]{1,0:T(32,128)(4,1)} %broadcast_compare_fusion, bf16[1024,4096]{1,0:T(8,128)(2,1)S(1)} %bitcast.18, bf16[4096,2048]{1,0:T(8,128)(2,1)} %get-tuple-element.13), kind=kOutput, calls=%fused_computation.2 | convolution fusion | flops 17184063488 | bytes 31457280 | tf_op jit(solution)/shard_map/dot_general | solution.py:351
  324.5 288.8 %share.1 = (bf16[1024,4096]{1,0:T(8,128)(2,1)}, bf16[1024,4096]{1,0:T(8,128)(2,1)}, bf16[4096,512]{1,0:T(8,128)(2,1)}) custom-call(bf16[1024,2048]{1,0:T(8,128)(2,1)} %select_convert_fusion.1.refs_0_, bf16[1024,2048]{1,0:T(8,128)(2,1)} %select_convert_fusion.refs_1_), custom_call_target="tpu_custom_call" | custom-call | tf_op jit(solution)/shard_map/share/pallas_call | solution.py:329
  613.3 0.0 copy-start.2
  613.3 8.3 %fusion = f32[1024,512]{1,0:T(8,128)S(1)} fusion(bf16[1024,4096]{1,0:T(8,128)(2,1)} %get-tuple-element.17, bf16[4096,2048]{1,0:T(8,128)(2,1)} %get-tuple-element.13, s32[]{:T(128)S(6)} %select_n.86), kind=kOutput, calls=%fused_computation.3 | convolution fusion | flops 4294967296 | bytes 14680068 | tf_op jit(solution)/shard_map/dot_general | solution.py:351
  621.6 0.0 copy-done.2
  621.6 0.0 copy-start
  621.7 0.0 copy-start.1
  621.7 7.2 %fusion.38 = f32[1024,512]{1,0:T(8,128)S(1)} fusion(bf16[1024,4096]{1,0:T(8,128)(2,1)} %get-tuple-element.12, bf16[4096,512]{1,0:T(8,128)(2,1)S(1)} %copy-done.2), kind=kOutput, calls=%fused_computation.67 | convolution fusion | flops 4294967296 | bytes 14680064 | tf_op jit(solution)/shard_map/dot_general | solution.py:351
  628.9 0.0 copy-done
  628.9 0.0 copy-done.1
  628.9 6.0 add_select_fusion
  (5 shorter events, 0.0 us)
Async XLA Ops:
  268.8 12.0 %slice-start = ((s8[8388608]{0:T(1024)(128)(4,1)}), s8[4194304]{0:T(1024)(128)(4,1)S(1)}, s32[]{:S(2)}) async-start(s8[8388608]{0:T(1024)(128)(4,1)} %bitcast.14), calls=%async_computation | async-start | bytes 8388608
  276.5 4.3 slice-start.1
  276.5 26.6 %slice-start.2 = ((s8[8388608]{0:T(1024)(128)(4,1)}), s8[4194304]{0:T(1024)(128)(4,1)S(1)}, s32[]{:S(2)}) async-start(s8[8388608]{0:T(1024)(128)(4,1)} %bitcast.17), calls=%async_computation.2 | async-start | bytes 8388608
  280.8 22.3 %slice-start.3 = ((s8[8388608]{0:T(1024)(128)(4,1)}), s8[4194304]{0:T(1024)(128)(4,1)S(1)}, s32[]{:S(2)}) async-start(s8[8388608]{0:T(1024)(128)(4,1)} %bitcast.17), calls=%async_computation.3 | async-start | bytes 8388608
  613.3 8.3 %copy-start.2 = (bf16[4096,512]{1,0:T(8,128)(2,1)S(1)}, bf16[4096,512]{1,0:T(8,128)(2,1)}, u32[]{:S(2)}) copy-start(bf16[4096,512]{1,0:T(8,128)(2,1)} %get-tuple-element.18) | copy-start | bytes 12582916
  621.6 7.3 %copy-start = (bf16[1024,4096]{1,0:T(8,128)(2,1)S(1)}, bf16[1024,4096]{1,0:T(8,128)(2,1)}, u32[]{:S(2)}) copy-start(bf16[1024,4096]{1,0:T(8,128)(2,1)} %get-tuple-element.15) | copy-start | bytes 25165828
  621.7 7.3 %copy-start.1 = (bf16[4096,512]{1,0:T(8,128)(2,1)S(1)}, bf16[4096,512]{1,0:T(8,128)(2,1)}, u32[]{:S(2)}) copy-start(bf16[4096,512]{1,0:T(8,128)(2,1)} %get-tuple-element.16) | copy-start | bytes 12582916

commit v2 on v1

--- a/solution.py
+++ b/solution.py
@@ -8,6 +8,8 @@
 BS = 128
 MESH = pl.DeviceIdType.MESH
 ANY = pl.BlockSpec(memory_space=pl.ANY)
+VMEM = pl.BlockSpec(memory_space=pltpu.VMEM)
+VMEM_LIMIT = 32 * 2**20
 
 
 def ring_place(index, size):
@@ -70,7 +72,7 @@
     return steps
 
 
-def gather_kernel(rows, cols, x_ref, g_ref, xr, xh, gr, gc, zs, zr, rs, rr, ss, sr, ls):
+def gather_kernel(rows, cols, x_ref, g_ref, xr, xh, gr, gh, gc, xs, gs, zs, zr, rs, rr, ss, sr, ls):
     spot = Spot(rows, cols)
     height, width = x_ref.shape
     c, l = spot.c, spot.l
@@ -90,8 +92,13 @@
     def g_view(row, first, count):
         return gc.at[pl.ds(pl.multiple_of(row * height + first, 16), count), :]
 
-    def x_mine(col):
-        return x_view(col)(spot.r, 0, height)
+    def slot(kind, col):
+        return (xs, gs)[kind].at[col]
+
+    def tile_of(kind, item):
+        if item[1] == 0:
+            return (x_ref, g_ref)[kind]
+        return slot(kind, col_of(item))
 
     spot.greet((spot.right, spot.left, spot.sibling, spot.up, spot.down))
 
@@ -119,10 +126,9 @@
 
     def line_copy(kind, way, d):
         col = c - d if way == 0 else c + d
-        own, view = (x_ref, x_mine) if kind == 0 else (g_ref, lambda k: wide(gr, k))
-        src = own if d == 0 else view(col)
+        src = tile_of(kind, (way, d))
         target = spot.up if way == 0 else spot.down
-        return remote(src, view(col), zs.at[kind, way, d], zr.at[kind, way, d], target)
+        return remote(src, slot(kind, col), zs.at[kind, way, d], zr.at[kind, way, d], target)
 
     def line_sends(way, d):
         further = c < cols - 1 if way == 0 else c > 0
@@ -130,43 +136,29 @@
 
     def sibling_copy(kind, item):
         i = index_of[item]
-        col = col_of(item)
-        if kind == 0:
-            src = x_ref if i == 0 else x_mine(col)
-            dst = wide(xr, col)
-        else:
-            src = g_ref if i == 0 else wide(gr, col)
-            dst = wide(gr, col)
-        return remote(src, dst, ss.at[kind, i], sr.at[kind, i], spot.sibling)
-
-    def sibling_arrival(kind, item):
-        return sibling_copy(kind, item)
-
-    def local_copy(item):
+        dst = wide((xr, gr)[kind], col_of(item))
+        return remote(tile_of(kind, item), dst, ss.at[kind, i], sr.at[kind, i], spot.sibling)
+
+    def local_copies(kind, item):
         i = index_of[item]
         col = col_of(item)
-        src = x_ref if i == 0 else x_mine(col)
-        return pltpu.make_async_copy(src, wide(xr, col), ls.at[i])
+        src = tile_of(kind, item)
+        if kind == 0:
+            targets = (wide(xr, col), x_view(col)(spot.r, 0, height))
+        else:
+            targets = (wide(gr, col), gh.at[:, pl.ds(pl.multiple_of(col * width, width), width)])
+        return [pltpu.make_async_copy(src, dst, ls.at[kind, j, i]) for j, dst in enumerate(targets)]
 
     def x_ring(item):
-        return ring_copies(
-            spot, x_view(col_of(item)), x_ref if item[1] == 0 else x_mine_ref(item), rs, rr, index_of[item]
-        )
-
-    def x_mine_ref(item):
-        return x_mine(col_of(item))
+        return ring_copies(spot, x_view(col_of(item)), tile_of(0, item), rs, rr, index_of[item])
 
     g_item = len(items)
 
     def g_ring():
         return ring_copies(spot, g_view, g_ref, rs, rr, g_item)
 
-    def own_copies():
-        return [
-            pltpu.make_async_copy(x_ref, x_mine(c), ls.at[len(items)]),
-            pltpu.make_async_copy(g_ref, wide(gr, c), ls.at[len(items) + 1]),
-            pltpu.make_async_copy(g_ref, g_view(spot.r, 0, height), ls.at[len(items) + 2]),
-        ]
+    def g_col_copy():
+        return pltpu.make_async_copy(g_ref, g_view(spot.r, 0, height), ls.at[0, 0, len(items)])
 
     def start_pair(pair):
         for copy in pair:
@@ -179,15 +171,18 @@
 
     ring_steps = rows // 2
 
+    def spread(kind, item):
+        sibling_copy(kind, item).start()
+        for copy in local_copies(kind, item):
+            copy.start()
+
     for way in (0, 1):
         when(line_sends(way, 0), lambda way=way: line_copy(0, way, 0).start())
     start_pair(x_ring((0, 0))[0])
     start_pair(g_ring()[0])
-    for copy in own_copies():
-        copy.start()
+    g_col_copy().start()
     for kind in (0, 1):
-        sibling_copy(kind, (0, 0)).start()
-    local_copy((0, 0)).start()
+        spread(kind, (0, 0))
     for way in (0, 1):
         when(line_sends(way, 0), lambda way=way: line_copy(1, way, 0).start())
 
@@ -196,14 +191,13 @@
         line_copy(0, way, d - 1).wait_recv()
         when(line_sends(way, d) if d < cols - 1 else jnp.bool_(False), lambda: line_copy(0, way, d).start())
         start_pair(x_ring(item)[0])
-        sibling_copy(0, item).start()
-        local_copy(item).start()
+        spread(0, item)
 
     def arrive_g(item):
         way, d = item
         line_copy(1, way, d - 1).wait_recv()
         when(line_sends(way, d) if d < cols - 1 else jnp.bool_(False), lambda: line_copy(1, way, d).start())
-        sibling_copy(1, item).start()
+        spread(1, item)
 
     def ring_on(item):
         steps = x_ring(item)
@@ -238,9 +232,11 @@
         for copy in steps[-1]:
             copy.wait_recv()
         for kind in (0, 1):
-            sibling_copy(kind, item).wait_send()
-            sibling_copy(kind, item).wait_recv()
-        local_copy(item).wait()
+            copy = sibling_copy(kind, item)
+            copy.wait_send()
+            copy.wait_recv()
+            for copy in local_copies(kind, item):
+                copy.wait()
 
     for item in items:
         when(there(item), lambda item=item: finish(item))
@@ -250,8 +246,7 @@
             copy.wait_send()
     for copy in steps[-1]:
         copy.wait_recv()
-    for copy in own_copies():
-        copy.wait()
+    g_col_copy().wait()
     for kind in (0, 1):
         for way in (0, 1):
             for d in range(cols - 1):
@@ -304,20 +299,23 @@
             shape(height, 2 * cols * width),
             shape(rows * height, cols * width),
             shape(height, 2 * cols * width),
+            shape(height, cols * width),
             shape(rows * height, width),
         ),
-        in_specs=[ANY] * 2,
-        out_specs=(ANY,) * 4,
+        in_specs=[VMEM] * 2,
+        out_specs=(ANY,) * 5,
         scratch_shapes=[
+            pltpu.VMEM((cols, height, width), x.dtype),
+            pltpu.VMEM((cols, height, width), x.dtype),
             dma((2, 2, cols)),
             dma((2, 2, cols)),
             dma((items + 1, rows // 2, 2)),
             dma((items + 1, rows // 2, 2)),
             dma((2, items)),
             dma((2, items)),
-            dma((items + 3,)),
+            dma((2, 2, items + 1)),
         ],
-        compiler_params=pltpu.CompilerParams(collective_id=0, has_side_effects=True),
+        compiler_params=pltpu.CompilerParams(collective_id=0, has_side_effects=True, vmem_limit_bytes=VMEM_LIMIT),
         name="gather_all",
     )(x, g)
 
@@ -333,7 +331,7 @@
             shape(height, 2 * cols * width),
             shape(rows * height, width),
         ),
-        in_specs=[ANY] * 2,
+        in_specs=[VMEM] * 2,
         out_specs=(ANY,) * 3,
         scratch_shapes=[
             dma((1, rows // 2, 2)),
@@ -342,7 +340,7 @@
             dma((2, cols)),
             dma((2 * cols + 1,)),
         ],
-        compiler_params=pltpu.CompilerParams(collective_id=1, has_side_effects=True),
+        compiler_params=pltpu.CompilerParams(collective_id=1, has_side_effects=True, vmem_limit_bytes=VMEM_LIMIT),
         name="share",
     )(s, p)
 
@@ -379,10 +377,7 @@
         half_mask = mask_of(block_pattern, row_at, half_at)
         xm = jnp.where(mask, density, jnp.zeros_like(density))
         masked_grad = jnp.where(mask, cotangent, jnp.zeros_like(cotangent))
-        x_rows, x_half, g_rows, g_cols = gather_all(rows, cols, xm, masked_grad)
-        g_half = lax.dynamic_index_in_dim(
-            g_rows.reshape(height, cols, layers, width), l, axis=2, keepdims=False
-        ).reshape(height, cols * width)
+        x_rows, x_half, g_rows, g_half, g_cols = gather_all(rows, cols, xm, masked_grad)
         square = jnp.where(half_mask, dot(x_rows, x_half), 0.0).astype(jnp.bfloat16)
         pulled = jnp.where(
             half_mask, 3.0 * g_half.astype(jnp.float32) - 2.0 * dot(g_rows, x_half), 0.0

time: 635 us -> 282 us (0.44)
  Pallas kernels: 519 us -> 214 us
  local copies, waits for them, and re-layouts: 33.8 us -> 0.8 us
  other arithmetic: 8.79 us -> 0.04 us
  matrix products: 73.7 us -> 67 us
    pallas_call x1, Pallas kernels: 289 us -> 37 us  [share(): pl.pallas_call(lambda *refs: share_kernel(rows, cols, width, *refs), out_...]
    pallas_call x1, Pallas kernels: 230 us -> 177 us  [gather_all(): pl.pallas_call(lambda *refs: gather_kernel(rows, cols, *refs), out_shape=...]
    reshape x1 -> x0, local copies, waits for them, and re-layouts: 14.5 us -> none  [per_device(): g_rows.reshape(height, cols, layers, width)]
    dynamic_slice x1 -> x0, local copies, waits for them, and re-layouts: 10.9 us -> none  [per_device(): lax.dynamic_index_in_dim(g_rows.reshape(height, cols, layers, width), l,...]
    mul x1 -> x0, other arithmetic: 8.75 us -> none  [per_device(): 3.0 * g_half.astype(jnp.float32) - 2.0 * dot(g_rows, x_half)]
    unnamed x15 -> x10, local copies, waits for them, and re-layouts: 7.69 us -> 0.03 us
where the time goes in v2:
time: 282 us
  Pallas kernels  214 us (76%)
  matrix products  67 us (24%)
    pallas_call x1, Pallas kernels, gather_all(): pl.pallas_call(lambda *refs: gather_kernel(rows, cols, *refs), out_shape=...  177 us
    dot_general x5, matrix products, dot(): return jnp.dot(a, b, preferred_element_type=jnp.float32)  62.8 us
    pallas_call x1, Pallas kernels, share(): pl.pallas_call(lambda *refs: share_kernel(rows, cols, width, *refs), out_...  37 us

profile of v2, /device:TPU:0, one launch (start us, length us, event | category | flops | bytes accessed | tf_op | source)
XLA Modules:
  0.0 282.1 jit_solution(11267895239943918924)
XLA Ops:
  0.0 0.8 slice_reduce_fusion
  0.8 0.0 copy-start.3
  0.8 0.0 copy-start.4
  0.8 3.0 %broadcast_compare_fusion = pred[1024,2048]{1,0:T(32,128)(4,1)S(1)} fusion(s32[2048]{0:T(1024)S(1)} %add_select_fusion.1, s32[362]{0:T(512)S(1)} %get-tuple-element.21, s32[1024]{0:T(1024)S(1)} %add_select_fusion.3, s32[362]{0:T(512)S(1)} %get-tuple-element.22), kind=kOutput, calls=%fused_computation.4 | convolution fusion | flops 1521547264 | bytes 2112336 | tf_op jit(solution)/shard_map/nr,nc->rc/dot_general | solution.py:357
  3.8 0.0 copy-done.3
  3.8 0.0 copy-done.4
  3.8 1.3 broadcast_select_fusion
  5.1 177.1 %gather_all.1 = (bf16[1024,4096]{1,0:T(8,128)(2,1)S(1)}, bf16[4096,2048]{1,0:T(8,128)(2,1)}, bf16[1024,4096]{1,0:T(8,128)(2,1)}, bf16[1024,2048]{1,0:T(8,128)(2,1)S(1)}, bf16[4096,512]{1,0:T(8,128)(2,1)S(1)}) custom-call(bf16[1024,512]{1,0:T(8,128)(2,1)S(1)} %get-tuple-element.24.refs_0_, bf16[1024,512]{1,0:T(8,128)(2,1)S(1)} %get-tuple-element.23.refs_1_), custom_call_target="tpu_custom_call" | custom-call | tf_op jit(solution)/shard_map/gather_all/pallas_call | solution.py:296
  182.2 0.0 copy-start
  182.2 25.1 %select_convert_fusion.refs_1_ = bf16[1024,2048]{1,0:T(8,128)(2,1)S(1)} fusion(pred[1024,2048]{1,0:T(32,128)(4,1)S(1)} %broadcast_compare_fusion, bf16[1024,2048]{1,0:T(8,128)(2,1)S(1)} %get-tuple-element.15, bf16[1024,4096]{1,0:T(8,128)(2,1)} %get-tuple-element.16, bf16[4096,2048]{1,0:T(8,128)(2,1)} %get-tuple-element.14), kind=kOutput, calls=%fused_computation | convolution fusion | flops 17192452096 | bytes 35651584 | tf_op jit(solution)/shard_map/dot_general | solution.py:349
  207.3 0.0 copy-done
  207.3 20.3 %select_convert_fusion.1.refs_0_ = bf16[1024,2048]{1,0:T(8,128)(2,1)S(1)} fusion(pred[1024,2048]{1,0:T(32,128)(4,1)S(1)} %broadcast_compare_fusion, bf16[1024,4096]{1,0:T(8,128)(2,1)S(1)} %get-tuple-element.13, bf16[4096,2048]{1,0:T(8,128)(2,1)} %get-tuple-element.14), kind=kOutput, calls=%fused_computation.1 | convolution fusion | flops 17184063488 | bytes 31457280 | tf_op jit(solution)/shard_map/dot_general | solution.py:349
  227.6 37.0 %share.1 = (bf16[1024,4096]{1,0:T(8,128)(2,1)S(1)}, bf16[1024,4096]{1,0:T(8,128)(2,1)}, bf16[4096,512]{1,0:T(8,128)(2,1)S(1)}) custom-call(bf16[1024,2048]{1,0:T(8,128)(2,1)S(1)} %select_convert_fusion.1.refs_0_, bf16[1024,2048]{1,0:T(8,128)(2,1)S(1)} %select_convert_fusion.refs_1_), custom_call_target="tpu_custom_call" | custom-call | tf_op jit(solution)/shard_map/share/pallas_call | solution.py:327
  264.6 0.0 copy-start.2
  264.6 4.5 %fusion.38 = f32[1024,512]{1,0:T(8,128)S(1)} fusion(bf16[1024,4096]{1,0:T(8,128)(2,1)S(1)} %get-tuple-element.13, bf16[4096,512]{1,0:T(8,128)(2,1)S(1)} %get-tuple-element.20), kind=kOutput, calls=%fused_computation.65 | convolution fusion | flops 4294967296 | bytes 14680064 | tf_op jit(solution)/shard_map/dot_general | solution.py:349
  269.1 0.0 copy-done.2
  269.1 0.0 copy-start.1
  269.1 6.9 %fusion = f32[1024,512]{1,0:T(8,128)S(1)} fusion(bf16[1024,4096]{1,0:T(8,128)(2,1)S(1)} %copy-done.2, bf16[4096,2048]{1,0:T(8,128)(2,1)} %get-tuple-element.14, s32[]{:T(128)S(6)} %select_n.81), kind=kOutput, calls=%fused_computation.2 | convolution fusion | flops 4294967296 | bytes 14680068 | tf_op jit(solution)/shard_map/dot_general | solution.py:349
  276.0 0.0 copy-done.1
  276.0 6.1 %add_select_fusion = f32[1024,512]{1,0:T(8,128)} fusion(pred[1024,512]{1,0:T(32,128)(4,1)S(1)} %get-tuple-element.25, f32[1024,512]{1,0:T(8,128)S(1)} %fusion.38, f32[1024,512]{1,0:T(8,128)S(1)} %fusion, bf16[1024,4096]{1,0:T(8,128)(2,1)S(1)} %get-tuple-element.17, bf16[4096,512]{1,0:T(8,128)(2,1)S(1)} %copy-done.1), kind=kOutput, calls=%fused_computation.6 | convolution fusion | flops 4297064448 | bytes 19398656 | tf_op jit(solution)/shard_map/dot_general | solution.py:349
  (3 shorter events, 0.0 us)
Async XLA Ops:
  0.8 3.0 %copy-start.3 = (bf16[1024,512]{1,0:T(8,128)(2,1)S(1)}, bf16[1024,512]{1,0:T(8,128)(2,1)}, u32[]{:S(2)}) copy-start(bf16[1024,512]{1,0:T(8,128)(2,1)} %param.4) | copy-start | bytes 3145732
  0.8 3.0 %copy-start.4 = (bf16[1024,512]{1,0:T(8,128)(2,1)S(1)}, bf16[1024,512]{1,0:T(8,128)(2,1)}, u32[]{:S(2)}) copy-start(bf16[1024,512]{1,0:T(8,128)(2,1)} %param.3) | copy-start | bytes 3145732
  182.2 25.1 %copy-start = (bf16[4096,512]{1,0:T(8,128)(2,1)}, bf16[4096,512]{1,0:T(8,128)(2,1)S(1)}, u32[]{:S(2)}) copy-start(bf16[4096,512]{1,0:T(8,128)(2,1)S(1)} %get-tuple-element.18) | copy-start | bytes 12582916
  264.6 4.5 %copy-start.2 = (bf16[1024,4096]{1,0:T(8,128)(2,1)S(1)}, bf16[1024,4096]{1,0:T(8,128)(2,1)}, u32[]{:S(2)}) copy-start(bf16[1024,4096]{1,0:T(8,128)(2,1)} %get-tuple-element.19) | copy-start | bytes 25165828
  269.1 6.9 %copy-start.1 = (bf16[4096,512]{1,0:T(8,128)(2,1)S(1)}, bf16[4096,512]{1,0:T(8,128)(2,1)}, u32[]{:S(2)}) copy-start(bf16[4096,512]{1,0:T(8,128)(2,1)} %copy-done) | copy-start | bytes 12582916

commit v3 on v2

--- a/solution.py
+++ b/solution.py
@@ -9,7 +9,7 @@
 MESH = pl.DeviceIdType.MESH
 ANY = pl.BlockSpec(memory_space=pl.ANY)
 VMEM = pl.BlockSpec(memory_space=pltpu.VMEM)
-VMEM_LIMIT = 32 * 2**20
+VMEM_LIMIT = 48 * 2**20
 
 
 def ring_place(index, size):
@@ -46,7 +46,7 @@
     )
 
 
-def ring_copies(spot, view, own, sends, recvs, item):
+def ring_copies(spot, view, own, sends, recvs, item, only=None):
     half_way = spot.rows // 2
     tile = own.shape[0]
     steps = []
@@ -59,20 +59,52 @@
             else:
                 first, count = way * (tile // 2), tile // 2
             src = own.at[pl.ds(first, count), :] if step == 1 else view(origin, first, count)
-            pair.append(
-                remote(
-                    src,
-                    view(origin, first, count),
-                    sends.at[item, step - 1, way],
-                    recvs.at[item, step - 1, way],
-                    target,
-                )
+            copy = remote(
+                src,
+                view(origin, first, count),
+                sends.at[item, step - 1, way],
+                recvs.at[item, step - 1, way],
+                target,
             )
+            if only is None:
+                pair.append((copy, None, None))
+            else:
+                pair.append((copy, origin == only, spot.at(-sign * step) == only))
         steps.append(pair)
     return steps
 
 
-def gather_kernel(rows, cols, x_ref, g_ref, xr, xh, gr, gh, gc, xs, gs, zs, zr, rs, rr, ss, sr, ls):
+def when(cond, body):
+    if cond is None:
+        body()
+    else:
+        pl.when(cond)(body)
+
+
+def start_pair(pair):
+    for copy, sent, _ in pair:
+        when(sent, copy.start)
+
+
+def pair_arrives(pair):
+    for copy, _, arrives in pair:
+        when(arrives, copy.wait_recv)
+
+
+def pair_left(pair):
+    for copy, sent, _ in pair:
+        when(sent, copy.wait_send)
+
+
+def pass_on(steps):
+    for step in range(1, len(steps)):
+        pair_arrives(steps[step - 1])
+        start_pair(steps[step])
+
+
+def gather_kernel(
+    rows, cols, x_ref, g_ref, xr, xh, gr, gh, gc, xs, gs, zs, zr, rs, rr, ss, sr, ls, *symmetric
+):
     spot = Spot(rows, cols)
     height, width = x_ref.shape
     c, l = spot.c, spot.l
@@ -114,12 +146,6 @@
         if d == 0:
             return None
         return c >= d if way == 0 else c < cols - d
-
-    def when(cond, body):
-        if cond is None:
-            body()
-        else:
-            pl.when(cond)(body)
 
     def both(a, b):
         return b if a is None else jnp.logical_and(a, b)
@@ -149,8 +175,112 @@
             targets = (wide(gr, col), gh.at[:, pl.ds(pl.multiple_of(col * width, width), width)])
         return [pltpu.make_async_copy(src, dst, ls.at[kind, j, i]) for j, dst in enumerate(targets)]
 
-    def x_ring(item):
-        return ring_copies(spot, x_view(col_of(item)), tile_of(0, item), rs, rr, index_of[item])
+    if symmetric:
+        rb, eb, tb, es, er, ts, tr, dl = symmetric
+
+    def sent_half(row, col):
+        return l + (row < col).astype(jnp.int32) * (1 - 2 * l)
+
+    def rows_at(tile, half):
+        return tile.at[pl.ds(pl.multiple_of(half * width, width), width), :]
+
+    def x_rings(item):
+        i, col, tile = index_of[item], col_of(item), tile_of(0, item)
+        if not symmetric:
+            return [ring_copies(spot, x_view(col), tile, rs, rr, i)]
+
+        def view(row, first, count):
+            return rb.at[row, col, pl.ds(first, count), :]
+
+        def extra_view(row, first, count):
+            return eb.at[col, pl.ds(first, count), :]
+
+        half = sent_half(spot.r, col)
+        return [
+            ring_copies(spot, view, rows_at(tile, half), rs, rr, i),
+            ring_copies(spot, extra_view, rows_at(tile, 1 - half), es, er, i, only=col),
+        ]
+
+    def x_start(item):
+        for steps in x_rings(item):
+            start_pair(steps[0])
+
+    def turned(item, offset, row):
+        i, col = index_of[item], col_of(item)
+        src = tb.at[row, col]
+        dst = xh.at[
+            pl.ds(pl.multiple_of(col * height + l * width, width), width),
+            pl.ds(pl.multiple_of(row * width, width), width),
+        ]
+        return (
+            pltpu.make_async_copy(src, dst, dl.at[1, offset, i]),
+            remote(src, dst, ts.at[offset, i], tr.at[offset, i], spot.sibling),
+        )
+
+    def placed(item, offset, row):
+        i, col = index_of[item], col_of(item)
+        half = sent_half(row, col)
+
+        def target(h):
+            return x_view(col)(row, h * width, width)
+
+        return (
+            pltpu.make_async_copy(rb.at[row, col], target(half), dl.at[0, offset, i]),
+            pltpu.make_async_copy(eb.at[col], target(1 - half), dl.at[2, 0, i]),
+        )
+
+    def turn(item, offset, row, src):
+        col = col_of(item)
+
+        @pl.when(jnp.logical_and(row != col, col != spot.r))
+        def _():
+            @pl.loop(0, width // BS)
+            def _(strip):
+                at = pl.ds(pl.multiple_of(strip * BS, BS), BS)
+                tb[row, col, at, :] = src[:, at].T
+
+            here, there_ = turned(item, offset, row)
+            pl.when(row > col)(here.start)
+            pl.when(row < col)(there_.start)
+
+    def turn_done(item, offset, row):
+        col = col_of(item)
+
+        @pl.when(jnp.logical_and(row != col, col != spot.r))
+        def _():
+            here, there_ = turned(item, offset, row)
+            pl.when(row > col)(here.wait)
+            pl.when(row < col)(there_.wait)
+
+    def turn_own(item):
+        if symmetric:
+            half = sent_half(spot.r, col_of(item))
+            turn(item, 0, spot.r, rows_at(tile_of(0, item), half))
+
+    def take(item):
+        for steps in x_rings(item):
+            pair_arrives(steps[-1])
+        if symmetric:
+
+            @pl.loop(1, rows)
+            def _(offset):
+                row = spot.at(offset)
+                tile, extra = placed(item, offset, row)
+                tile.start()
+                pl.when(row == col_of(item))(extra.start)
+                turn(item, offset, row, rb.at[row, col_of(item)])
+
+    def take_done(item):
+        if symmetric:
+            turn_done(item, 0, spot.r)
+
+            @pl.loop(1, rows)
+            def _(offset):
+                row = spot.at(offset)
+                tile, extra = placed(item, offset, row)
+                tile.wait()
+                pl.when(row == col_of(item))(extra.wait)
+                turn_done(item, offset, row)
 
     g_item = len(items)
 
@@ -159,17 +289,6 @@
 
     def g_col_copy():
         return pltpu.make_async_copy(g_ref, g_view(spot.r, 0, height), ls.at[0, 0, len(items)])
-
-    def start_pair(pair):
-        for copy in pair:
-            copy.start()
-
-    def forward(steps, step):
-        for way in (0, 1):
-            steps[step - 1][way].wait_recv()
-        start_pair(steps[step])
-
-    ring_steps = rows // 2
 
     def spread(kind, item):
         sibling_copy(kind, item).start()
@@ -178,7 +297,7 @@
 
     for way in (0, 1):
         when(line_sends(way, 0), lambda way=way: line_copy(0, way, 0).start())
-    start_pair(x_ring((0, 0))[0])
+    x_start((0, 0))
     start_pair(g_ring()[0])
     g_col_copy().start()
     for kind in (0, 1):
@@ -190,7 +309,7 @@
         way, d = item
         line_copy(0, way, d - 1).wait_recv()
         when(line_sends(way, d) if d < cols - 1 else jnp.bool_(False), lambda: line_copy(0, way, d).start())
-        start_pair(x_ring(item)[0])
+        x_start(item)
         spread(0, item)
 
     def arrive_g(item):
@@ -200,37 +319,34 @@
         spread(1, item)
 
     def ring_on(item):
-        steps = x_ring(item)
-        for step in range(1, ring_steps):
-            forward(steps, step)
-
-    def g_ring_on():
-        steps = g_ring()
-        for step in range(1, ring_steps):
-            forward(steps, step)
+        for steps in x_rings(item):
+            pass_on(steps)
+
+    turn_own((0, 0))
+    previous = [(0, 0)]
+    def each(some, body):
+        for item in some:
+            when(there(item), lambda item=item: body(item))
 
     for d in range(1, cols):
-        for way in (0, 1):
-            when(there((way, d)), lambda way=way, d=d: arrive_x((way, d)))
+        current = [(0, d), (1, d)]
+        each(current, arrive_x)
+        each(previous, ring_on)
         if d == 1:
-            ring_on((0, 0))
-            g_ring_on()
-        else:
-            for way in (0, 1):
-                when(there((way, d - 1)), lambda way=way, d=d: ring_on((way, d - 1)))
-        for way in (0, 1):
-            when(there((way, d)), lambda way=way, d=d: arrive_g((way, d)))
-    for way in (0, 1):
-        when(there((way, cols - 1)), lambda way=way: ring_on((way, cols - 1)))
+            pass_on(g_ring())
+        each(current, turn_own)
+        each(current, arrive_g)
+        each(previous, take)
+        previous = current
+    each(previous, ring_on)
+    each(previous, take)
 
     def finish(item):
         way, d = item
-        steps = x_ring(item)
-        for step in range(ring_steps):
-            for copy in steps[step]:
-                copy.wait_send()
-        for copy in steps[-1]:
-            copy.wait_recv()
+        for steps in x_rings(item):
+            for pair in steps:
+                pair_left(pair)
+        take_done(item)
         for kind in (0, 1):
             copy = sibling_copy(kind, item)
             copy.wait_send()
@@ -238,14 +354,11 @@
             for copy in local_copies(kind, item):
                 copy.wait()
 
-    for item in items:
-        when(there(item), lambda item=item: finish(item))
+    each(items, finish)
     steps = g_ring()
-    for step in range(ring_steps):
-        for copy in steps[step]:
-            copy.wait_send()
-    for copy in steps[-1]:
-        copy.wait_recv()
+    for pair in steps:
+        pair_left(pair)
+    pair_arrives(steps[-1])
     g_col_copy().wait()
     for kind in (0, 1):
         for way in (0, 1):
@@ -263,8 +376,7 @@
         return pc.at[pl.ds(pl.multiple_of(row * height + first, 16), count), :]
 
     steps = ring_copies(spot, view, mine, rs, rr, 0)
-    for copy in steps[0]:
-        copy.start()
+    start_pair(steps[0])
     others = [pltpu.make_async_copy(mine, view(spot.r, 0, height), ls.at[2 * cols])]
     for kind, (half, full) in enumerate(((p_ref, pf), (s_ref, sf))):
         for col in range(cols):
@@ -274,16 +386,10 @@
             others.append(pltpu.make_async_copy(src, dst, ls.at[kind * cols + col]))
     for copy in others:
         copy.start()
-    for step in range(1, len(steps)):
-        for copy in steps[step - 1]:
-            copy.wait_recv()
-        for copy in steps[step]:
-            copy.start()
-    for copy in steps[-1]:
-        copy.wait_recv()
+    pass_on(steps)
+    pair_arrives(steps[-1])
     for pair in steps:
-        for copy in pair:
-            copy.wait_send()
+        pair_left(pair)
     for copy in others:
         copy.wait()
 
@@ -293,6 +399,18 @@
     shape = lambda a, b: jax.ShapeDtypeStruct((a, b), x.dtype)
     items = 2 * cols - 1
     dma = pltpu.SemaphoreType.DMA
+    symmetric = []
+    if height == 2 * width and rows == cols:
+        symmetric = [
+            pltpu.VMEM((rows, cols, width, width), x.dtype),
+            pltpu.VMEM((cols, width, width), x.dtype),
+            pltpu.VMEM((rows, cols, width, width), x.dtype),
+            dma((items, rows // 2, 2)),
+            dma((items, rows // 2, 2)),
+            dma((rows, items)),
+            dma((rows, items)),
+            dma((3, rows, items)),
+        ]
     return pl.pallas_call(
         lambda *refs: gather_kernel(rows, cols, *refs),
         out_shape=(
@@ -314,6 +432,7 @@
             dma((2, items)),
             dma((2, items)),
             dma((2, 2, items + 1)),
+            *symmetric,
         ],
         compiler_params=pltpu.CompilerParams(collective_id=0, has_side_effects=True, vmem_limit_bytes=VMEM_LIMIT),
         name="gather_all",

time: 282 us -> 279 us (0.989)
    pallas_call x1, Pallas kernels: 177 us -> 171 us  [gather_all(): pl.pallas_call(lambda *refs: gather_kernel(rows, cols, *refs), out_shape=...]
    pallas_call x1, Pallas kernels: 37 us -> 41.6 us  [share(): pl.pallas_call(lambda *refs: share_kernel(rows, cols, width, *refs), out_...]
where the time goes in v3:
time: 279 us
  Pallas kernels  212 us (76%)
  matrix products  65.6 us (24%)
    pallas_call x1, Pallas kernels, gather_all(): pl.pallas_call(lambda *refs: gather_kernel(rows, cols, *refs), out_shape=...  171 us
    dot_general x5, matrix products, dot(): return jnp.dot(a, b, preferred_element_type=jnp.float32)  61.3 us
    pallas_call x1, Pallas kernels, share(): pl.pallas_call(lambda *refs: share_kernel(rows, cols, width, *refs), out_...  41.6 us

profile of v3, /device:TPU:0, one launch (start us, length us, event | category | flops | bytes accessed | tf_op | source)
XLA Modules:
  0.0 279.1 jit_solution(18010848412170921587)
XLA Ops:
  0.0 0.8 slice_reduce_fusion
  0.8 0.0 copy-start.4
  0.8 0.0 copy-start.5
  0.8 3.0 %broadcast_compare_fusion = pred[1024,2048]{1,0:T(32,128)(4,1)S(1)} fusion(s32[2048]{0:T(1024)S(1)} %add_select_fusion.1, s32[362]{0:T(512)S(1)} %get-tuple-element.21, s32[1024]{0:T(1024)S(1)} %add_select_fusion.3, s32[362]{0:T(512)S(1)} %get-tuple-element.22), kind=kOutput, calls=%fused_computation.4 | convolution fusion | flops 1521547264 | bytes 2112336 | tf_op jit(solution)/shard_map/nr,nc->rc/dot_general | solution.py:476
  3.8 0.0 copy-done.4
  3.8 0.0 copy-done.5
  3.8 1.3 broadcast_select_fusion
  5.1 170.9 %gather_all.1 = (bf16[1024,4096]{1,0:T(8,128)(2,1)}, bf16[4096,2048]{1,0:T(8,128)(2,1)}, bf16[1024,4096]{1,0:T(8,128)(2,1)}, bf16[1024,2048]{1,0:T(8,128)(2,1)}, bf16[4096,512]{1,0:T(8,128)(2,1)}) custom-call(bf16[1024,512]{1,0:T(8,128)(2,1)S(1)} %get-tuple-element.24.refs_0_, bf16[1024,512]{1,0:T(8,128)(2,1)S(1)} %get-tuple-element.23.refs_1_), custom_call_target="tpu_custom_call" | custom-call | tf_op jit(solution)/shard_map/gather_all/pallas_call | solution.py:414
  176.1 0.0 copy-start
  176.1 0.0 copy-start.1
  176.1 25.0 %select_convert_fusion.refs_1_ = bf16[1024,2048]{1,0:T(8,128)(2,1)} fusion(pred[1024,2048]{1,0:T(32,128)(4,1)S(1)} %broadcast_compare_fusion, bf16[1024,2048]{1,0:T(8,128)(2,1)} %get-tuple-element.15, bf16[1024,4096]{1,0:T(8,128)(2,1)} %get-tuple-element.16, bf16[4096,2048]{1,0:T(8,128)(2,1)} %get-tuple-element.14), kind=kOutput, calls=%fused_computation | convolution fusion | flops 17192452096 | bytes 35651584 | tf_op jit(solution)/shard_map/dot_general | solution.py:468
  201.1 0.0 copy-done
  201.1 0.0 copy-done.1
  201.1 19.1 %select_convert_fusion.1.refs_0_ = bf16[1024,2048]{1,0:T(8,128)(2,1)} fusion(pred[1024,2048]{1,0:T(32,128)(4,1)S(1)} %broadcast_compare_fusion, bf16[1024,4096]{1,0:T(8,128)(2,1)S(1)} %copy-done.1, bf16[4096,2048]{1,0:T(8,128)(2,1)S(1)} %copy-done), kind=kOutput, calls=%fused_computation.1 | convolution fusion | flops 17184063488 | bytes 31457280 | tf_op jit(solution)/shard_map/dot_general | solution.py:468
  220.2 41.6 %share.1 = (bf16[1024,4096]{1,0:T(8,128)(2,1)}, bf16[1024,4096]{1,0:T(8,128)(2,1)}, bf16[4096,512]{1,0:T(8,128)(2,1)S(1)}) custom-call(bf16[1024,2048]{1,0:T(8,128)(2,1)} %select_convert_fusion.1.refs_0_, bf16[1024,2048]{1,0:T(8,128)(2,1)} %select_convert_fusion.refs_1_), custom_call_target="tpu_custom_call" | custom-call | tf_op jit(solution)/shard_map/share/pallas_call | solution.py:446
  261.8 0.0 copy-start.2
  261.8 0.0 slice-start
  261.8 4.5 %fusion.38 = f32[1024,512]{1,0:T(8,128)S(1)} fusion(bf16[1024,4096]{1,0:T(8,128)(2,1)S(1)} %copy-done.1, bf16[4096,512]{1,0:T(8,128)(2,1)S(1)} %get-tuple-element.20), kind=kOutput, calls=%fused_computation.65 | convolution fusion | flops 4294967296 | bytes 14680064 | tf_op jit(solution)/shard_map/dot_general | solution.py:468
  266.3 0.0 copy-done.2
  266.3 0.0 slice-start.1
  266.3 0.0 copy-start.3
  266.3 6.7 %fusion = f32[1024,512]{1,0:T(8,128)S(1)} fusion(bf16[1024,4096]{1,0:T(8,128)(2,1)S(1)} %copy-done.2, bf16[4096,2048]{1,0:T(8,128)(2,1)} %get-tuple-element.14, s32[]{:T(128)S(6)} %select_n.81), kind=kOutput, calls=%fused_computation.2 | convolution fusion | flops 4294967296 | bytes 14680068 | tf_op jit(solution)/shard_map/dot_general | solution.py:468
  273.0 0.0 slice-done
  273.0 0.0 slice-done.1
  273.0 0.0 copy-done.3
  273.1 6.0 %add_select_fusion = f32[1024,512]{1,0:T(8,128)} fusion(pred[1024,512]{1,0:T(32,128)(4,1)S(1)} %get-tuple-element.25, f32[1024,512]{1,0:T(8,128)S(1)} %fusion.38, f32[1024,512]{1,0:T(8,128)S(1)} %fusion, bf16[1024,4096]{1,0:T(8,128)(2,1)S(1)} %bitcast.10, bf16[4096,512]{1,0:T(8,128)(2,1)S(1)} %copy-done.3), kind=kOutput, calls=%fused_computation.6 | convolution fusion | flops 4297064448 | bytes 19398656 | tf_op jit(solution)/shard_map/dot_general | solution.py:468
  (4 shorter events, 0.0 us)
Async XLA Ops:
  0.8 3.0 %copy-start.4 = (bf16[1024,512]{1,0:T(8,128)(2,1)S(1)}, bf16[1024,512]{1,0:T(8,128)(2,1)}, u32[]{:S(2)}) copy-start(bf16[1024,512]{1,0:T(8,128)(2,1)} %param.4) | copy-start | bytes 3145732
  0.8 3.0 %copy-start.5 = (bf16[1024,512]{1,0:T(8,128)(2,1)S(1)}, bf16[1024,512]{1,0:T(8,128)(2,1)}, u32[]{:S(2)}) copy-start(bf16[1024,512]{1,0:T(8,128)(2,1)} %param.3) | copy-start | bytes 3145732
  176.1 25.1 %copy-start = (bf16[4096,2048]{1,0:T(8,128)(2,1)S(1)}, bf16[4096,2048]{1,0:T(8,128)(2,1)}, u32[]{:S(2)}) copy-start(bf16[4096,2048]{1,0:T(8,128)(2,1)} %get-tuple-element.14) | copy-start | bytes 50331652
  176.1 25.0 %copy-start.1 = (bf16[1024,4096]{1,0:T(8,128)(2,1)S(1)}, bf16[1024,4096]{1,0:T(8,128)(2,1)}, u32[]{:S(2)}) copy-start(bf16[1024,4096]{1,0:T(8,128)(2,1)} %get-tuple-element.13) | copy-start | bytes 25165828
  261.8 4.5 %copy-start.2 = (bf16[1024,4096]{1,0:T(8,128)(2,1)S(1)}, bf16[1024,4096]{1,0:T(8,128)(2,1)}, u32[]{:S(2)}) copy-start(bf16[1024,4096]{1,0:T(8,128)(2,1)} %get-tuple-element.19) | copy-start | bytes 25165828
  261.8 11.2 %slice-start = ((s8[8388608]{0:T(1024)(128)(4,1)}), s8[4194304]{0:T(1024)(128)(4,1)S(1)}, s32[]{:S(2)}) async-start(s8[8388608]{0:T(1024)(128)(4,1)} %bitcast.9), calls=%async_computation | async-start | bytes 8388608
  266.3 6.7 %slice-start.1 = ((s8[8388608]{0:T(1024)(128)(4,1)}), s8[4194304]{0:T(1024)(128)(4,1)S(1)}, s32[]{:S(2)}) async-start(s8[8388608]{0:T(1024)(128)(4,1)} %bitcast.9), calls=%async_computation.1 | async-start | bytes 8388608
  266.3 6.7 %copy-start.3 = (bf16[4096,512]{1,0:T(8,128)(2,1)S(1)}, bf16[4096,512]{1,0:T(8,128)(2,1)}, u32[]{:S(2)}) copy-start(bf16[4096,512]{1,0:T(8,128)(2,1)} %get-tuple-element.18) | copy-start | bytes 12582916

commit v4 on v3

--- a/solution.py
+++ b/solution.py
@@ -302,13 +302,19 @@
     g_col_copy().start()
     for kind in (0, 1):
         spread(kind, (0, 0))
+
+    def line_g_start(way, d):
+        last = (c if way == 0 else cols - 1 - c) == d
+        when(both(line_sends(way, 0), last), line_copy(1, way, 0).start)
+
     for way in (0, 1):
-        when(line_sends(way, 0), lambda way=way: line_copy(1, way, 0).start())
+        line_g_start(way, 0)
 
     def arrive_x(item):
         way, d = item
         line_copy(0, way, d - 1).wait_recv()
         when(line_sends(way, d) if d < cols - 1 else jnp.bool_(False), lambda: line_copy(0, way, d).start())
+        line_g_start(way, d)
         x_start(item)
         spread(0, item)
 
@@ -335,11 +341,16 @@
         if d == 1:
             pass_on(g_ring())
         each(current, turn_own)
-        each(current, arrive_g)
         each(previous, take)
         previous = current
+    each([(0, 1), (1, 1)], arrive_g)
     each(previous, ring_on)
-    each(previous, take)
+    for d in range(2, cols):
+        each([(0, d), (1, d)], arrive_g)
+        if d == 2:
+            each(previous, take)
+    if cols < 3:
+        each(previous, take)
 
     def finish(item):
         way, d = item

time: 279 us -> 290 us (1.039)
  Pallas kernels: 212 us -> 223 us
    pallas_call x1, Pallas kernels: 171 us -> 182 us  [gather_all(): pl.pallas_call(lambda *refs: gather_kernel(rows, cols, *refs), out_shape=...]
where the time goes in v4:
time: 290 us
  Pallas kernels  223 us (77%)
  matrix products  65.6 us (23%)
    pallas_call x1, Pallas kernels, gather_all(): pl.pallas_call(lambda *refs: gather_kernel(rows, cols, *refs), out_shape=...  182 us
    dot_general x5, matrix products, dot(): return jnp.dot(a, b, preferred_element_type=jnp.float32)  61.3 us
    pallas_call x1, Pallas kernels, share(): pl.pallas_call(lambda *refs: share_kernel(rows, cols, width, *refs), out_...  41.4 us

profile of v4, /device:TPU:0, one launch (start us, length us, event | category | flops | bytes accessed | tf_op | source)
XLA Modules:
  0.0 289.8 jit_solution(13882574981480140475)
XLA Ops:
  0.0 0.8 slice_reduce_fusion
  0.8 0.0 copy-start.4
  0.8 0.0 copy-start.5
  0.8 3.0 %broadcast_compare_fusion = pred[1024,2048]{1,0:T(32,128)(4,1)S(1)} fusion(s32[2048]{0:T(1024)S(1)} %add_select_fusion.1, s32[362]{0:T(512)S(1)} %get-tuple-element.21, s32[1024]{0:T(1024)S(1)} %add_select_fusion.3, s32[362]{0:T(512)S(1)} %get-tuple-element.22), kind=kOutput, calls=%fused_computation.4 | convolution fusion | flops 1521547264 | bytes 2112336 | tf_op jit(solution)/shard_map/nr,nc->rc/dot_general | solution.py:487
  3.8 0.0 copy-done.4
  3.8 0.0 copy-done.5
  3.8 1.3 broadcast_select_fusion
  5.1 181.9 %gather_all.1 = (bf16[1024,4096]{1,0:T(8,128)(2,1)}, bf16[4096,2048]{1,0:T(8,128)(2,1)}, bf16[1024,4096]{1,0:T(8,128)(2,1)}, bf16[1024,2048]{1,0:T(8,128)(2,1)}, bf16[4096,512]{1,0:T(8,128)(2,1)}) custom-call(bf16[1024,512]{1,0:T(8,128)(2,1)S(1)} %get-tuple-element.24.refs_0_, bf16[1024,512]{1,0:T(8,128)(2,1)S(1)} %get-tuple-element.23.refs_1_), custom_call_target="tpu_custom_call" | custom-call | tf_op jit(solution)/shard_map/gather_all/pallas_call | solution.py:425
  187.0 0.0 copy-start
  187.0 0.0 copy-start.1
  187.0 25.0 %select_convert_fusion.refs_1_ = bf16[1024,2048]{1,0:T(8,128)(2,1)} fusion(pred[1024,2048]{1,0:T(32,128)(4,1)S(1)} %broadcast_compare_fusion, bf16[1024,2048]{1,0:T(8,128)(2,1)} %get-tuple-element.15, bf16[1024,4096]{1,0:T(8,128)(2,1)} %get-tuple-element.16, bf16[4096,2048]{1,0:T(8,128)(2,1)} %get-tuple-element.14), kind=kOutput, calls=%fused_computation | convolution fusion | flops 17192452096 | bytes 35651584 | tf_op jit(solution)/shard_map/dot_general | solution.py:479
  212.0 0.0 copy-done
  212.1 0.0 copy-done.1
  212.1 19.1 %select_convert_fusion.1.refs_0_ = bf16[1024,2048]{1,0:T(8,128)(2,1)} fusion(pred[1024,2048]{1,0:T(32,128)(4,1)S(1)} %broadcast_compare_fusion, bf16[1024,4096]{1,0:T(8,128)(2,1)S(1)} %copy-done.1, bf16[4096,2048]{1,0:T(8,128)(2,1)S(1)} %copy-done), kind=kOutput, calls=%fused_computation.1 | convolution fusion | flops 17184063488 | bytes 31457280 | tf_op jit(solution)/shard_map/dot_general | solution.py:479
  231.2 41.4 %share.1 = (bf16[1024,4096]{1,0:T(8,128)(2,1)}, bf16[1024,4096]{1,0:T(8,128)(2,1)}, bf16[4096,512]{1,0:T(8,128)(2,1)S(1)}) custom-call(bf16[1024,2048]{1,0:T(8,128)(2,1)} %select_convert_fusion.1.refs_0_, bf16[1024,2048]{1,0:T(8,128)(2,1)} %select_convert_fusion.refs_1_), custom_call_target="tpu_custom_call" | custom-call | tf_op jit(solution)/shard_map/share/pallas_call | solution.py:457
  272.6 0.0 copy-start.2
  272.6 0.0 slice-start
  272.6 4.5 %fusion.38 = f32[1024,512]{1,0:T(8,128)S(1)} fusion(bf16[1024,4096]{1,0:T(8,128)(2,1)S(1)} %copy-done.1, bf16[4096,512]{1,0:T(8,128)(2,1)S(1)} %get-tuple-element.20), kind=kOutput, calls=%fused_computation.65 | convolution fusion | flops 4294967296 | bytes 14680064 | tf_op jit(solution)/shard_map/dot_general | solution.py:479
  277.1 0.0 copy-done.2
  277.1 0.0 slice-start.1
  277.1 0.0 copy-start.3
  277.1 6.7 %fusion = f32[1024,512]{1,0:T(8,128)S(1)} fusion(bf16[1024,4096]{1,0:T(8,128)(2,1)S(1)} %copy-done.2, bf16[4096,2048]{1,0:T(8,128)(2,1)} %get-tuple-element.14, s32[]{:T(128)S(6)} %select_n.81), kind=kOutput, calls=%fused_computation.2 | convolution fusion | flops 4294967296 | bytes 14680068 | tf_op jit(solution)/shard_map/dot_general | solution.py:479
  283.8 0.0 slice-done
  283.8 0.0 slice-done.1
  283.8 0.0 copy-done.3
  283.8 6.0 %add_select_fusion = f32[1024,512]{1,0:T(8,128)} fusion(pred[1024,512]{1,0:T(32,128)(4,1)S(1)} %get-tuple-element.25, f32[1024,512]{1,0:T(8,128)S(1)} %fusion.38, f32[1024,512]{1,0:T(8,128)S(1)} %fusion, bf16[1024,4096]{1,0:T(8,128)(2,1)S(1)} %bitcast.10, bf16[4096,512]{1,0:T(8,128)(2,1)S(1)} %copy-done.3), kind=kOutput, calls=%fused_computation.6 | convolution fusion | flops 4297064448 | bytes 19398656 | tf_op jit(solution)/shard_map/dot_general | solution.py:479
  (4 shorter events, 0.0 us)
Async XLA Ops:
  0.8 3.0 %copy-start.4 = (bf16[1024,512]{1,0:T(8,128)(2,1)S(1)}, bf16[1024,512]{1,0:T(8,128)(2,1)}, u32[]{:S(2)}) copy-start(bf16[1024,512]{1,0:T(8,128)(2,1)} %param.4) | copy-start | bytes 3145732
  0.8 3.0 %copy-start.5 = (bf16[1024,512]{1,0:T(8,128)(2,1)S(1)}, bf16[1024,512]{1,0:T(8,128)(2,1)}, u32[]{:S(2)}) copy-start(bf16[1024,512]{1,0:T(8,128)(2,1)} %param.3) | copy-start | bytes 3145732
  187.0 25.1 %copy-start = (bf16[4096,2048]{1,0:T(8,128)(2,1)S(1)}, bf16[4096,2048]{1,0:T(8,128)(2,1)}, u32[]{:S(2)}) copy-start(bf16[4096,2048]{1,0:T(8,128)(2,1)} %get-tuple-element.14) | copy-start | bytes 50331652
  187.0 25.1 %copy-start.1 = (bf16[1024,4096]{1,0:T(8,128)(2,1)S(1)}, bf16[1024,4096]{1,0:T(8,128)(2,1)}, u32[]{:S(2)}) copy-start(bf16[1024,4096]{1,0:T(8,128)(2,1)} %get-tuple-element.13) | copy-start | bytes 25165828
  272.6 4.5 %copy-start.2 = (bf16[1024,4096]{1,0:T(8,128)(2,1)S(1)}, bf16[1024,4096]{1,0:T(8,128)(2,1)}, u32[]{:S(2)}) copy-start(bf16[1024,4096]{1,0:T(8,128)(2,1)} %get-tuple-element.19) | copy-start | bytes 25165828
  272.6 11.2 %slice-start = ((s8[8388608]{0:T(1024)(128)(4,1)}), s8[4194304]{0:T(1024)(128)(4,1)S(1)}, s32[]{:S(2)}) async-start(s8[8388608]{0:T(1024)(128)(4,1)} %bitcast.9), calls=%async_computation | async-start | bytes 8388608
  277.1 6.7 %slice-start.1 = ((s8[8388608]{0:T(1024)(128)(4,1)}), s8[4194304]{0:T(1024)(128)(4,1)S(1)}, s32[]{:S(2)}) async-start(s8[8388608]{0:T(1024)(128)(4,1)} %bitcast.9), calls=%async_computation.1 | async-start | bytes 8388608
  277.1 6.7 %copy-start.3 = (bf16[4096,512]{1,0:T(8,128)(2,1)S(1)}, bf16[4096,512]{1,0:T(8,128)(2,1)}, u32[]{:S(2)}) copy-start(bf16[4096,512]{1,0:T(8,128)(2,1)} %get-tuple-element.18) | copy-start | bytes 12582916

commit v5 on v3

--- a/solution.py
+++ b/solution.py
@@ -302,9 +302,6 @@
     g_col_copy().start()
     for kind in (0, 1):
         spread(kind, (0, 0))
-    for way in (0, 1):
-        when(line_sends(way, 0), lambda way=way: line_copy(1, way, 0).start())
-
     def arrive_x(item):
         way, d = item
         line_copy(0, way, d - 1).wait_recv()
@@ -331,15 +328,20 @@
     for d in range(1, cols):
         current = [(0, d), (1, d)]
         each(current, arrive_x)
+        if d == 1:
+            for way in (0, 1):
+                when(line_sends(way, 0), line_copy(1, way, 0).start)
+        else:
+            each([(0, d - 1), (1, d - 1)], arrive_g)
         each(previous, ring_on)
         if d == 1:
             pass_on(g_ring())
         each(current, turn_own)
-        each(current, arrive_g)
         each(previous, take)
         previous = current
     each(previous, ring_on)
     each(previous, take)
+    each(previous, arrive_g)
 
     def finish(item):
         way, d = item

time: 279 us -> 267 us (0.957)
  Pallas kernels: 212 us -> 200 us
    pallas_call x1, Pallas kernels: 171 us -> 157 us  [gather_all(): pl.pallas_call(lambda *refs: gather_kernel(rows, cols, *refs), out_shape=...]
where the time goes in v5:
time: 267 us
  Pallas kernels  200 us (75%)
  matrix products  65.6 us (25%)
    pallas_call x1, Pallas kernels, gather_all(): pl.pallas_call(lambda *refs: gather_kernel(rows, cols, *refs), out_shape=...  157 us
    dot_general x5, matrix products, dot(): return jnp.dot(a, b, preferred_element_type=jnp.float32)  61.3 us
    pallas_call x1, Pallas kernels, share(): pl.pallas_call(lambda *refs: share_kernel(rows, cols, width, *refs), out_...  43.3 us

profile of v5, /device:TPU:0, one launch (start us, length us, event | category | flops | bytes accessed | tf_op | source)
XLA Modules:
  0.0 267.0 jit_solution(1544681205542780457)
XLA Ops:
  0.0 0.8 slice_reduce_fusion
  0.8 0.0 copy-start.4
  0.8 0.0 copy-start.5
  0.8 3.0 %broadcast_compare_fusion = pred[1024,2048]{1,0:T(32,128)(4,1)S(1)} fusion(s32[2048]{0:T(1024)S(1)} %add_select_fusion.1, s32[362]{0:T(512)S(1)} %get-tuple-element.21, s32[1024]{0:T(1024)S(1)} %add_select_fusion.3, s32[362]{0:T(512)S(1)} %get-tuple-element.22), kind=kOutput, calls=%fused_computation.4 | convolution fusion | flops 1521547264 | bytes 2112336 | tf_op jit(solution)/shard_map/nr,nc->rc/dot_general | solution.py:478
  3.8 0.0 copy-done.4
  3.8 0.0 copy-done.5
  3.8 1.3 broadcast_select_fusion
  5.1 157.2 %gather_all.1 = (bf16[1024,4096]{1,0:T(8,128)(2,1)}, bf16[4096,2048]{1,0:T(8,128)(2,1)}, bf16[1024,4096]{1,0:T(8,128)(2,1)}, bf16[1024,2048]{1,0:T(8,128)(2,1)}, bf16[4096,512]{1,0:T(8,128)(2,1)}) custom-call(bf16[1024,512]{1,0:T(8,128)(2,1)S(1)} %get-tuple-element.24.refs_0_, bf16[1024,512]{1,0:T(8,128)(2,1)S(1)} %get-tuple-element.23.refs_1_), custom_call_target="tpu_custom_call" | custom-call | tf_op jit(solution)/shard_map/gather_all/pallas_call | solution.py:416
  162.3 0.0 copy-start
  162.3 0.0 copy-start.1
  162.3 25.0 %select_convert_fusion.refs_1_ = bf16[1024,2048]{1,0:T(8,128)(2,1)} fusion(pred[1024,2048]{1,0:T(32,128)(4,1)S(1)} %broadcast_compare_fusion, bf16[1024,2048]{1,0:T(8,128)(2,1)} %get-tuple-element.15, bf16[1024,4096]{1,0:T(8,128)(2,1)} %get-tuple-element.16, bf16[4096,2048]{1,0:T(8,128)(2,1)} %get-tuple-element.14), kind=kOutput, calls=%fused_computation | convolution fusion | flops 17192452096 | bytes 35651584 | tf_op jit(solution)/shard_map/dot_general | solution.py:470
  187.3 0.0 copy-done
  187.3 0.0 copy-done.1
  187.3 19.1 %select_convert_fusion.1.refs_0_ = bf16[1024,2048]{1,0:T(8,128)(2,1)} fusion(pred[1024,2048]{1,0:T(32,128)(4,1)S(1)} %broadcast_compare_fusion, bf16[1024,4096]{1,0:T(8,128)(2,1)S(1)} %copy-done.1, bf16[4096,2048]{1,0:T(8,128)(2,1)S(1)} %copy-done), kind=kOutput, calls=%fused_computation.1 | convolution fusion | flops 17184063488 | bytes 31457280 | tf_op jit(solution)/shard_map/dot_general | solution.py:470
  206.4 43.3 %share.1 = (bf16[1024,4096]{1,0:T(8,128)(2,1)}, bf16[1024,4096]{1,0:T(8,128)(2,1)}, bf16[4096,512]{1,0:T(8,128)(2,1)S(1)}) custom-call(bf16[1024,2048]{1,0:T(8,128)(2,1)} %select_convert_fusion.1.refs_0_, bf16[1024,2048]{1,0:T(8,128)(2,1)} %select_convert_fusion.refs_1_), custom_call_target="tpu_custom_call" | custom-call | tf_op jit(solution)/shard_map/share/pallas_call | solution.py:448
  249.7 0.0 copy-start.2
  249.7 0.0 slice-start
  249.7 4.5 %fusion.38 = f32[1024,512]{1,0:T(8,128)S(1)} fusion(bf16[1024,4096]{1,0:T(8,128)(2,1)S(1)} %copy-done.1, bf16[4096,512]{1,0:T(8,128)(2,1)S(1)} %get-tuple-element.20), kind=kOutput, calls=%fused_computation.65 | convolution fusion | flops 4294967296 | bytes 14680064 | tf_op jit(solution)/shard_map/dot_general | solution.py:470
  254.2 0.0 copy-done.2
  254.2 0.0 slice-start.1
  254.2 0.0 copy-start.3
  254.3 6.7 %fusion = f32[1024,512]{1,0:T(8,128)S(1)} fusion(bf16[1024,4096]{1,0:T(8,128)(2,1)S(1)} %copy-done.2, bf16[4096,2048]{1,0:T(8,128)(2,1)} %get-tuple-element.14, s32[]{:T(128)S(6)} %select_n.81), kind=kOutput, calls=%fused_computation.2 | convolution fusion | flops 4294967296 | bytes 14680068 | tf_op jit(solution)/shard_map/dot_general | solution.py:470
  260.9 0.0 slice-done
  260.9 0.0 slice-done.1
  261.0 0.0 copy-done.3
  261.0 6.0 %add_select_fusion = f32[1024,512]{1,0:T(8,128)} fusion(pred[1024,512]{1,0:T(32,128)(4,1)S(1)} %get-tuple-element.25, f32[1024,512]{1,0:T(8,128)S(1)} %fusion.38, f32[1024,512]{1,0:T(8,128)S(1)} %fusion, bf16[1024,4096]{1,0:T(8,128)(2,1)S(1)} %bitcast.10, bf16[4096,512]{1,0:T(8,128)(2,1)S(1)} %copy-done.3), kind=kOutput, calls=%fused_computation.6 | convolution fusion | flops 4297064448 | bytes 19398656 | tf_op jit(solution)/shard_map/dot_general | solution.py:470
  (4 shorter events, 0.0 us)
Async XLA Ops:
  0.8 3.0 %copy-start.4 = (bf16[1024,512]{1,0:T(8,128)(2,1)S(1)}, bf16[1024,512]{1,0:T(8,128)(2,1)}, u32[]{:S(2)}) copy-start(bf16[1024,512]{1,0:T(8,128)(2,1)} %param.4) | copy-start | bytes 3145732
  0.8 3.0 %copy-start.5 = (bf16[1024,512]{1,0:T(8,128)(2,1)S(1)}, bf16[1024,512]{1,0:T(8,128)(2,1)}, u32[]{:S(2)}) copy-start(bf16[1024,512]{1,0:T(8,128)(2,1)} %param.3) | copy-start | bytes 3145732
  162.3 25.1 %copy-start = (bf16[4096,2048]{1,0:T(8,128)(2,1)S(1)}, bf16[4096,2048]{1,0:T(8,128)(2,1)}, u32[]{:S(2)}) copy-start(bf16[4096,2048]{1,0:T(8,128)(2,1)} %get-tuple-element.14) | copy-start | bytes 50331652
  162.3 25.0 %copy-start.1 = (bf16[1024,4096]{1,0:T(8,128)(2,1)S(1)}, bf16[1024,4096]{1,0:T(8,128)(2,1)}, u32[]{:S(2)}) copy-start(bf16[1024,4096]{1,0:T(8,128)(2,1)} %get-tuple-element.13) | copy-start | bytes 25165828
  249.7 4.5 %copy-start.2 = (bf16[1024,4096]{1,0:T(8,128)(2,1)S(1)}, bf16[1024,4096]{1,0:T(8,128)(2,1)}, u32[]{:S(2)}) copy-start(bf16[1024,4096]{1,0:T(8,128)(2,1)} %get-tuple-element.19) | copy-start | bytes 25165828
  249.7 11.2 %slice-start = ((s8[8388608]{0:T(1024)(128)(4,1)}), s8[4194304]{0:T(1024)(128)(4,1)S(1)}, s32[]{:S(2)}) async-start(s8[8388608]{0:T(1024)(128)(4,1)} %bitcast.9), calls=%async_computation | async-start | bytes 8388608
  254.2 6.7 %slice-start.1 = ((s8[8388608]{0:T(1024)(128)(4,1)}), s8[4194304]{0:T(1024)(128)(4,1)S(1)}, s32[]{:S(2)}) async-start(s8[8388608]{0:T(1024)(128)(4,1)} %bitcast.9), calls=%async_computation.1 | async-start | bytes 8388608
  254.2 6.7 %copy-start.3 = (bf16[4096,512]{1,0:T(8,128)(2,1)S(1)}, bf16[4096,512]{1,0:T(8,128)(2,1)}, u32[]{:S(2)}) copy-start(bf16[4096,512]{1,0:T(8,128)(2,1)} %get-tuple-element.18) | copy-start | bytes 12582916

commit v6 on v5

--- a/solution.py
+++ b/solution.py
@@ -368,10 +368,21 @@
                 when(line_sends(way, d), lambda kind=kind, way=way, d=d: line_copy(kind, way, d).wait_send())
 
 
-def share_kernel(rows, cols, width, s_ref, p_ref, sf, pf, pc, rs, rr, ss, sr, ls):
+def share_kernel(
+    rows, cols, width, p_ref, mask_ref, xr, xh, sf, pf, pc, left, right, square, rs, rr, ss, sr, ls, fs
+):
     spot = Spot(rows, cols)
-    height = s_ref.shape[0]
+    height = p_ref.shape[0]
     spot.greet((spot.right, spot.left, spot.sibling))
+
+    def fetch(col):
+        slot = lax.rem(col, 2)
+        src = xh.at[:, pl.ds(pl.multiple_of(col * width, width), width)]
+        return pltpu.make_async_copy(src, right.at[slot], fs.at[slot])
+
+    whole_left = pltpu.make_async_copy(xr, left, fs.at[2])
+    whole_left.start()
+    fetch(jnp.int32(0)).start()
     mine = p_ref.at[:, pl.ds(pl.multiple_of(spot.c * width, width), width)]
 
     def view(row, first, count):
@@ -379,21 +390,54 @@
 
     steps = ring_copies(spot, view, mine, rs, rr, 0)
     start_pair(steps[0])
-    others = [pltpu.make_async_copy(mine, view(spot.r, 0, height), ls.at[2 * cols])]
-    for kind, (half, full) in enumerate(((p_ref, pf), (s_ref, sf))):
-        for col in range(cols):
-            src = half.at[:, pl.ds(col * width, width)]
-            dst = full.at[:, pl.ds(pl.multiple_of((col * 2 + spot.l) * width, width), width)]
-            others.append(remote(src, dst, ss.at[kind, col], sr.at[kind, col], spot.sibling))
-            others.append(pltpu.make_async_copy(src, dst, ls.at[kind * cols + col]))
-    for copy in others:
-        copy.start()
+    own_cols = pltpu.make_async_copy(mine, view(spot.r, 0, height), ls.at[2, 0])
+    own_cols.start()
+
+    def spread(kind, col):
+        at = pl.ds(pl.multiple_of(col * width, width), width)
+        src = p_ref.at[:, at] if kind == 0 else square.at[col]
+        dst = (pf, sf)[kind].at[:, pl.ds(pl.multiple_of((col * 2 + spot.l) * width, width), width)]
+        return (
+            remote(src, dst, ss.at[kind, col], sr.at[kind, col], spot.sibling),
+            pltpu.make_async_copy(src, dst, ls.at[kind, col]),
+        )
+
+    @pl.loop(0, cols)
+    def _(col):
+        for copy in spread(0, col):
+            copy.start()
+
+    whole_left.wait()
+    block = min(2 * BS, height)
+
+    @pl.loop(0, cols)
+    def _(col):
+        fetch(col).wait()
+        pl.when(col + 1 < cols)(lambda: fetch(col + 1).start())
+        slot = lax.rem(col, 2)
+        at = pl.ds(pl.multiple_of(col * width, width), width)
+
+        @pl.loop(0, height // block)
+        def _(part):
+            these = pl.ds(pl.multiple_of(part * block, block), block)
+            product = jnp.dot(left[these, :], right[slot], preferred_element_type=jnp.float32)
+            kept = jnp.where(mask_ref[these, at] > 0, product, 0.0)
+            square[col, these, :] = kept.astype(square.dtype)
+
+        for copy in spread(1, col):
+            copy.start()
+
     pass_on(steps)
     pair_arrives(steps[-1])
     for pair in steps:
         pair_left(pair)
-    for copy in others:
-        copy.wait()
+    own_cols.wait()
+
+    @pl.loop(0, cols)
+    def _(col):
+        for kind in (0, 1):
+            for copy in spread(kind, col):
+                copy.wait()
 
 
 def gather_all(rows, cols, x, g):
@@ -441,9 +485,10 @@
     )(x, g)
 
 
-def share(rows, cols, width, s, p):
-    height = s.shape[0]
-    shape = lambda a, b: jax.ShapeDtypeStruct((a, b), s.dtype)
+def share(rows, cols, width, p, mask, x_rows, x_half):
+    height = p.shape[0]
+    depth = x_half.shape[0]
+    shape = lambda a, b: jax.ShapeDtypeStruct((a, b), p.dtype)
     dma = pltpu.SemaphoreType.DMA
     return pl.pallas_call(
         lambda *refs: share_kernel(rows, cols, width, *refs),
@@ -452,18 +497,24 @@
             shape(height, 2 * cols * width),
             shape(rows * height, width),
         ),
-        in_specs=[VMEM] * 2,
+        in_specs=[VMEM, VMEM, ANY, ANY],
         out_specs=(ANY,) * 3,
         scratch_shapes=[
+            pltpu.VMEM((height, depth), p.dtype),
+            pltpu.VMEM((2, depth, width), p.dtype),
+            pltpu.VMEM((cols, height, width), p.dtype),
             dma((1, rows // 2, 2)),
             dma((1, rows // 2, 2)),
             dma((2, cols)),
             dma((2, cols)),
-            dma((2 * cols + 1,)),
+            dma((3, cols)),
+            dma((3,)),
         ],
-        compiler_params=pltpu.CompilerParams(collective_id=1, has_side_effects=True, vmem_limit_bytes=VMEM_LIMIT),
+        compiler_params=pltpu.CompilerParams(
+            collective_id=1, has_side_effects=True, vmem_limit_bytes=VMEM_LIMIT
+        ),
         name="share",
-    )(s, p)
+    )(p, mask, x_rows, x_half)
 
 
 def dot(a, b):
@@ -499,11 +550,12 @@
         xm = jnp.where(mask, density, jnp.zeros_like(density))
         masked_grad = jnp.where(mask, cotangent, jnp.zeros_like(cotangent))
         x_rows, x_half, g_rows, g_half, g_cols = gather_all(rows, cols, xm, masked_grad)
-        square = jnp.where(half_mask, dot(x_rows, x_half), 0.0).astype(jnp.bfloat16)
         pulled = jnp.where(
             half_mask, 3.0 * g_half.astype(jnp.float32) - 2.0 * dot(g_rows, x_half), 0.0
         ).astype(jnp.bfloat16)
-        s_rows, p_rows, p_cols = share(rows, cols, width, square, pulled)
+        s_rows, p_rows, p_cols = share(
+            rows, cols, width, pulled, half_mask.astype(jnp.bfloat16), x_rows, x_half
+        )
         x_cols = lax.dynamic_slice_in_dim(x_half, c * width, width, axis=1)
         total = -2.0 * dot(s_rows, g_cols) + dot(p_rows, x_cols) + dot(x_rows, p_cols)
         return jnp.where(mask, total, 0.0)

time: 267 us -> 254 us (0.951)
  matrix products: 65.6 us -> 50.1 us
    dot_general x5 -> x4, matrix products: 61.3 us -> 42.3 us  [dot(): return jnp.dot(a, b, preferred_element_type=jnp.float32)]
    dot_general x2, matrix products: 4.22 us -> 7.8 us  [mask_of(): jnp.einsum('nr,nc->rc', hits(block_pattern[0], row_positions), hits(block...]
where the time goes in v6:
time: 254 us
  Pallas kernels  202 us (80%)
  matrix products  50.1 us (20%)
    pallas_call x1, Pallas kernels, gather_all(): pl.pallas_call(lambda *refs: gather_kernel(rows, cols, *refs), out_shape=...  157 us
    pallas_call x1, Pallas kernels, share(): pl.pallas_call(lambda *refs: share_kernel(rows, cols, width, *refs), out_...  45.4 us
    dot_general x4, matrix products, dot(): return jnp.dot(a, b, preferred_element_type=jnp.float32)  42.3 us
    dot_general x2, matrix products, mask_of(): jnp.einsum('nr,nc->rc', hits(block_pattern[0], row_positions), hits(block...  7.8 us

profile of v6, /device:TPU:0, one launch (start us, length us, event | category | flops | bytes accessed | tf_op | source)
XLA Modules:
  0.0 253.5 jit_solution(17358428186393389575)
XLA Ops:
  0.0 0.8 slice_reduce_fusion
  0.8 2.8 %broadcast_select_fusion = (bf16[1024,512]{1,0:T(8,128)(2,1)S(1)}, bf16[1024,512]{1,0:T(8,128)(2,1)S(1)}, pred[1024,512]{1,0:T(32,128)(4,1)S(1)}) fusion(bf16[1024,512]{1,0:T(8,128)(2,1)} %param.4, bf16[1024,512]{1,0:T(8,128)(2,1)} %param.3, s32[512]{0:T(512)S(1)} %add_select_fusion.4, s32[362]{0:T(512)S(1)} %get-tuple-element.21, ...), kind=kOutput, calls=%fused_computation.17 | convolution fusion | flops 381713408 | bytes 4727632 | tf_op jit(solution)/shard_map/nr,nc->rc/dot_general | solution.py:529
  3.6 5.0 %fusion.38 = (bf16[1024,2048]{1,0:T(8,128)(2,1)}, pred[1024,2048]{1,0:T(32,128)(4,1)S(1)}) fusion(s32[2048]{0:T(1024)S(1)} %add_select_fusion.1, s32[362]{0:T(512)S(1)} %get-tuple-element.21, s32[1024]{0:T(1024)S(1)} %add_select_fusion.3, s32[362]{0:T(512)S(1)} %get-tuple-element.22), kind=kOutput, calls=%fused_computation.64 | convolution fusion | flops 1523644416 | bytes 6306640 | tf_op jit(solution)/shard_map/nr,nc->rc/dot_general | solution.py:529
  8.6 157.1 %gather_all.1 = (bf16[1024,4096]{1,0:T(8,128)(2,1)}, bf16[4096,2048]{1,0:T(8,128)(2,1)}, bf16[1024,4096]{1,0:T(8,128)(2,1)}, bf16[1024,2048]{1,0:T(8,128)(2,1)}, bf16[4096,512]{1,0:T(8,128)(2,1)}) custom-call(bf16[1024,512]{1,0:T(8,128)(2,1)S(1)} %get-tuple-element.24.refs_0_, bf16[1024,512]{1,0:T(8,128)(2,1)S(1)} %get-tuple-element.23.refs_1_), custom_call_target="tpu_custom_call" | custom-call | tf_op jit(solution)/shard_map/gather_all/pallas_call | solution.py:460
  165.7 24.9 %select_convert_fusion.refs_0_ = bf16[1024,2048]{1,0:T(8,128)(2,1)} fusion(pred[1024,2048]{1,0:T(32,128)(4,1)S(1)} %get-tuple-element.27, bf16[1024,2048]{1,0:T(8,128)(2,1)} %get-tuple-element.13, bf16[1024,4096]{1,0:T(8,128)(2,1)} %get-tuple-element.14, bf16[4096,2048]{1,0:T(8,128)(2,1)} %get-tuple-element.15.refs_3_), kind=kOutput, calls=%fused_computation | convolution fusion | flops 17192452096 | bytes 35651584 | tf_op jit(solution)/shard_map/dot_general | solution.py:521
  190.6 0.0 copy-start
  190.6 45.4 %share.1 = (bf16[1024,4096]{1,0:T(8,128)(2,1)}, bf16[1024,4096]{1,0:T(8,128)(2,1)}, bf16[4096,512]{1,0:T(8,128)(2,1)S(1)}) custom-call(bf16[1024,2048]{1,0:T(8,128)(2,1)} %select_convert_fusion.refs_0_, bf16[1024,2048]{1,0:T(8,128)(2,1)} %get-tuple-element.26.refs_1_, bf16[1024,4096]{1,0:T(8,128)(2,1)} %get-tuple-element.16.refs_2_, ...), custom_call_target="tpu_custom_call" | custom-call | tf_op jit(solution)/shard_map/share/pallas_call | solution.py:493
  236.0 0.0 copy-done
  236.0 0.0 copy-start.1
  236.0 0.0 slice-start
  236.0 4.5 %fusion.39 = f32[1024,512]{1,0:T(8,128)S(1)} fusion(bf16[1024,4096]{1,0:T(8,128)(2,1)S(1)} %copy-done, bf16[4096,512]{1,0:T(8,128)(2,1)S(1)} %get-tuple-element.20), kind=kOutput, calls=%fused_computation.65 | convolution fusion | flops 4294967296 | bytes 14680064 | tf_op jit(solution)/shard_map/dot_general | solution.py:521
  240.5 0.0 copy-done.1
  240.5 0.0 slice-start.1
  240.5 0.0 copy-start.2
  240.6 6.9 %fusion = f32[1024,512]{1,0:T(8,128)S(1)} fusion(bf16[1024,4096]{1,0:T(8,128)(2,1)S(1)} %copy-done.1, bf16[4096,2048]{1,0:T(8,128)(2,1)} %get-tuple-element.15.refs_3_, s32[]{:T(128)S(6)} %select_n.77), kind=kOutput, calls=%fused_computation.1 | convolution fusion | flops 4294967296 | bytes 14680068 | tf_op jit(solution)/shard_map/dot_general | solution.py:521
  247.5 0.0 slice-done
  247.5 0.0 slice-done.1
  247.5 0.0 copy-done.2
  247.5 6.0 %add_select_fusion = f32[1024,512]{1,0:T(8,128)} fusion(pred[1024,512]{1,0:T(32,128)(4,1)S(1)} %get-tuple-element.25, f32[1024,512]{1,0:T(8,128)S(1)} %fusion.39, f32[1024,512]{1,0:T(8,128)S(1)} %fusion, bf16[1024,4096]{1,0:T(8,128)(2,1)S(1)} %bitcast.8, bf16[4096,512]{1,0:T(8,128)(2,1)S(1)} %copy-done.2), kind=kOutput, calls=%fused_computation.5 | convolution fusion | flops 4297064448 | bytes 19398656 | tf_op jit(solution)/shard_map/dot_general | solution.py:521
  (4 shorter events, 0.0 us)
Async XLA Ops:
  190.6 45.4 %copy-start = (bf16[1024,4096]{1,0:T(8,128)(2,1)S(1)}, bf16[1024,4096]{1,0:T(8,128)(2,1)}, u32[]{:S(2)}) copy-start(bf16[1024,4096]{1,0:T(8,128)(2,1)} %get-tuple-element.16.refs_2_) | copy-start | bytes 25165828
  236.0 4.5 %copy-start.1 = (bf16[1024,4096]{1,0:T(8,128)(2,1)S(1)}, bf16[1024,4096]{1,0:T(8,128)(2,1)}, u32[]{:S(2)}) copy-start(bf16[1024,4096]{1,0:T(8,128)(2,1)} %get-tuple-element.19) | copy-start | bytes 25165828
  236.0 11.4 %slice-start = ((s8[8388608]{0:T(1024)(128)(4,1)}), s8[4194304]{0:T(1024)(128)(4,1)S(1)}, s32[]{:S(2)}) async-start(s8[8388608]{0:T(1024)(128)(4,1)} %bitcast.7), calls=%async_computation | async-start | bytes 8388608
  240.5 6.9 %slice-start.1 = ((s8[8388608]{0:T(1024)(128)(4,1)}), s8[4194304]{0:T(1024)(128)(4,1)S(1)}, s32[]{:S(2)}) async-start(s8[8388608]{0:T(1024)(128)(4,1)} %bitcast.7), calls=%async_computation.1 | async-start | bytes 8388608
  240.5 6.9 %copy-start.2 = (bf16[4096,512]{1,0:T(8,128)(2,1)S(1)}, bf16[4096,512]{1,0:T(8,128)(2,1)}, u32[]{:S(2)}) copy-start(bf16[4096,512]{1,0:T(8,128)(2,1)} %get-tuple-element.18) | copy-start | bytes 12582916

commit v7 on v6

--- a/solution.py
+++ b/solution.py
@@ -410,8 +410,7 @@
     whole_left.wait()
     block = min(2 * BS, height)
 
-    @pl.loop(0, cols)
-    def _(col):
+    def square_block(col):
         fetch(col).wait()
         pl.when(col + 1 < cols)(lambda: fetch(col + 1).start())
         slot = lax.rem(col, 2)
@@ -427,7 +426,9 @@
         for copy in spread(1, col):
             copy.start()
 
+    pl.loop(0, cols - 1)(square_block)
     pass_on(steps)
+    square_block(jnp.int32(cols - 1))
     pair_arrives(steps[-1])
     for pair in steps:
         pair_left(pair)

time: 254 us -> 252 us (level)
  no operation moved by 1% of the time
where the time goes in v7:
time: 252 us
  Pallas kernels  201 us (80%)
  matrix products  50.1 us (20%)
    pallas_call x1, Pallas kernels, gather_all(): pl.pallas_call(lambda *refs: gather_kernel(rows, cols, *refs), out_shape=...  157 us
    pallas_call x1, Pallas kernels, share(): pl.pallas_call(lambda *refs: share_kernel(rows, cols, width, *refs), out_...  43.4 us
    dot_general x4, matrix products, dot(): return jnp.dot(a, b, preferred_element_type=jnp.float32)  42.3 us
    dot_general x2, matrix products, mask_of(): jnp.einsum('nr,nc->rc', hits(block_pattern[0], row_positions), hits(block...  7.8 us

profile of v7, /device:TPU:0, one launch (start us, length us, event | category | flops | bytes accessed | tf_op | source)
XLA Modules:
  0.0 251.6 jit_solution(9948344853924313572)
XLA Ops:
  0.0 0.8 slice_reduce_fusion
  0.8 2.8 %broadcast_select_fusion = (bf16[1024,512]{1,0:T(8,128)(2,1)S(1)}, bf16[1024,512]{1,0:T(8,128)(2,1)S(1)}, pred[1024,512]{1,0:T(32,128)(4,1)S(1)}) fusion(bf16[1024,512]{1,0:T(8,128)(2,1)} %param.4, bf16[1024,512]{1,0:T(8,128)(2,1)} %param.3, s32[512]{0:T(512)S(1)} %add_select_fusion.4, s32[362]{0:T(512)S(1)} %get-tuple-element.21, ...), kind=kOutput, calls=%fused_computation.17 | convolution fusion | flops 381713408 | bytes 4727632 | tf_op jit(solution)/shard_map/nr,nc->rc/dot_general | solution.py:530
  3.6 5.0 %fusion.38 = (bf16[1024,2048]{1,0:T(8,128)(2,1)}, pred[1024,2048]{1,0:T(32,128)(4,1)S(1)}) fusion(s32[2048]{0:T(1024)S(1)} %add_select_fusion.1, s32[362]{0:T(512)S(1)} %get-tuple-element.21, s32[1024]{0:T(1024)S(1)} %add_select_fusion.3, s32[362]{0:T(512)S(1)} %get-tuple-element.22), kind=kOutput, calls=%fused_computation.64 | convolution fusion | flops 1523644416 | bytes 6306640 | tf_op jit(solution)/shard_map/nr,nc->rc/dot_general | solution.py:530
  8.6 157.1 %gather_all.1 = (bf16[1024,4096]{1,0:T(8,128)(2,1)}, bf16[4096,2048]{1,0:T(8,128)(2,1)}, bf16[1024,4096]{1,0:T(8,128)(2,1)}, bf16[1024,2048]{1,0:T(8,128)(2,1)}, bf16[4096,512]{1,0:T(8,128)(2,1)}) custom-call(bf16[1024,512]{1,0:T(8,128)(2,1)S(1)} %get-tuple-element.24.refs_0_, bf16[1024,512]{1,0:T(8,128)(2,1)S(1)} %get-tuple-element.23.refs_1_), custom_call_target="tpu_custom_call" | custom-call | tf_op jit(solution)/shard_map/gather_all/pallas_call | solution.py:461
  165.7 24.9 %select_convert_fusion.refs_0_ = bf16[1024,2048]{1,0:T(8,128)(2,1)} fusion(pred[1024,2048]{1,0:T(32,128)(4,1)S(1)} %get-tuple-element.27, bf16[1024,2048]{1,0:T(8,128)(2,1)} %get-tuple-element.13, bf16[1024,4096]{1,0:T(8,128)(2,1)} %get-tuple-element.14, bf16[4096,2048]{1,0:T(8,128)(2,1)} %get-tuple-element.15.refs_3_), kind=kOutput, calls=%fused_computation | convolution fusion | flops 17192452096 | bytes 35651584 | tf_op jit(solution)/shard_map/dot_general | solution.py:522
  190.6 0.0 copy-start
  190.6 43.4 %share.1 = (bf16[1024,4096]{1,0:T(8,128)(2,1)}, bf16[1024,4096]{1,0:T(8,128)(2,1)}, bf16[4096,512]{1,0:T(8,128)(2,1)S(1)}) custom-call(bf16[1024,2048]{1,0:T(8,128)(2,1)} %select_convert_fusion.refs_0_, bf16[1024,2048]{1,0:T(8,128)(2,1)} %get-tuple-element.26.refs_1_, bf16[1024,4096]{1,0:T(8,128)(2,1)} %get-tuple-element.16.refs_2_, ...), custom_call_target="tpu_custom_call" | custom-call | tf_op jit(solution)/shard_map/share/pallas_call | solution.py:494
  234.1 0.0 copy-done
  234.1 0.0 copy-start.1
  234.1 0.0 slice-start
  234.1 4.5 %fusion.39 = f32[1024,512]{1,0:T(8,128)S(1)} fusion(bf16[1024,4096]{1,0:T(8,128)(2,1)S(1)} %copy-done, bf16[4096,512]{1,0:T(8,128)(2,1)S(1)} %get-tuple-element.20), kind=kOutput, calls=%fused_computation.65 | convolution fusion | flops 4294967296 | bytes 14680064 | tf_op jit(solution)/shard_map/dot_general | solution.py:522
  238.6 0.0 copy-done.1
  238.6 0.0 slice-start.1
  238.6 0.0 copy-start.2
  238.6 6.9 %fusion = f32[1024,512]{1,0:T(8,128)S(1)} fusion(bf16[1024,4096]{1,0:T(8,128)(2,1)S(1)} %copy-done.1, bf16[4096,2048]{1,0:T(8,128)(2,1)} %get-tuple-element.15.refs_3_, s32[]{:T(128)S(6)} %select_n.77), kind=kOutput, calls=%fused_computation.1 | convolution fusion | flops 4294967296 | bytes 14680068 | tf_op jit(solution)/shard_map/dot_general | solution.py:522
  245.5 0.0 slice-done
  245.5 0.0 slice-done.1
  245.5 0.0 copy-done.2
  245.5 6.0 %add_select_fusion = f32[1024,512]{1,0:T(8,128)} fusion(pred[1024,512]{1,0:T(32,128)(4,1)S(1)} %get-tuple-element.25, f32[1024,512]{1,0:T(8,128)S(1)} %fusion.39, f32[1024,512]{1,0:T(8,128)S(1)} %fusion, bf16[1024,4096]{1,0:T(8,128)(2,1)S(1)} %bitcast.8, bf16[4096,512]{1,0:T(8,128)(2,1)S(1)} %copy-done.2), kind=kOutput, calls=%fused_computation.5 | convolution fusion | flops 4297064448 | bytes 19398656 | tf_op jit(solution)/shard_map/dot_general | solution.py:522
  (4 shorter events, 0.0 us)
Async XLA Ops:
  190.6 43.4 %copy-start = (bf16[1024,4096]{1,0:T(8,128)(2,1)S(1)}, bf16[1024,4096]{1,0:T(8,128)(2,1)}, u32[]{:S(2)}) copy-start(bf16[1024,4096]{1,0:T(8,128)(2,1)} %get-tuple-element.16.refs_2_) | copy-start | bytes 25165828
  234.1 4.5 %copy-start.1 = (bf16[1024,4096]{1,0:T(8,128)(2,1)S(1)}, bf16[1024,4096]{1,0:T(8,128)(2,1)}, u32[]{:S(2)}) copy-start(bf16[1024,4096]{1,0:T(8,128)(2,1)} %get-tuple-element.19) | copy-start | bytes 25165828
  234.1 11.4 %slice-start = ((s8[8388608]{0:T(1024)(128)(4,1)}), s8[4194304]{0:T(1024)(128)(4,1)S(1)}, s32[]{:S(2)}) async-start(s8[8388608]{0:T(1024)(128)(4,1)} %bitcast.7), calls=%async_computation | async-start | bytes 8388608
  238.6 6.9 %slice-start.1 = ((s8[8388608]{0:T(1024)(128)(4,1)}), s8[4194304]{0:T(1024)(128)(4,1)S(1)}, s32[]{:S(2)}) async-start(s8[8388608]{0:T(1024)(128)(4,1)} %bitcast.7), calls=%async_computation.1 | async-start | bytes 8388608
  238.6 6.9 %copy-start.2 = (bf16[4096,512]{1,0:T(8,128)(2,1)S(1)}, bf16[4096,512]{1,0:T(8,128)(2,1)}, u32[]{:S(2)}) copy-start(bf16[4096,512]{1,0:T(8,128)(2,1)} %get-tuple-element.18) | copy-start | bytes 12582916
